TPU v7x, 128 devices: a whole 4x4x4 slice. The times are simulated.
128 devices in a mesh: row: 8 (over z, core), col: 16 (over y, x).
Axes of the slice: x: 4, y: 4, z: 4, core: 2. Of those that a mesh axis runs over, the one named last changes fastest.
Arguments:
- features: bfloat16 [131072, 256], P(('row', 'col')), may hold values from -6 to 6
- zorder_to: int32 [131072], P(('row', 'col')), may hold values from 0 to 131071, as said below
- hilbert_from: int32 [131072], P(('row', 'col')), may hold values from 0 to 131071, as said below
- qkv_weight: bfloat16 [256, 768], replicated, may hold values from -3 to 3, as said below
- proj_weight: bfloat16 [256, 256], replicated, may hold values from -0.375 to 0.375
- out_grad: bfloat16 [131072, 256], P(('row', 'col')), may hold values from -6 to 6
Outputs:
- block_out: bfloat16 [131072, 256], P(('row', 'col'))
- feature_grad: bfloat16 [131072, 256], P(('row', 'col'))
- qkv_grad: float32 [256, 768], replicated
- proj_grad: float32 [256, 256], replicated
Inputs may be any that keep to these rules, and one draw needn't show every extreme that they name: zorder_to is a permutation and hilbert_from is its inverse. The points at the z-order positions of one block of 1024 go to every block of 1024 Hilbert positions, exactly 8 points to each. `hilbert_from`: the inverse of zorder_to. `qkv_weight`: value columns have entries of order 256 ** -0.5 times a few; query and key columns may be up to 4 times larger.
All inputs are finite; a program needn't handle non-finite values.
Results may differ from a plain program's by a relative error of at most 0.007.
The roundings to bfloat16 on the way count: a program that leaves them out, or rounds other values in their place, can miss the bound.
Values may be sent and summed in bfloat16 or wider, within the bound.
A program may use at most 128 MiB of HBM per device.

v0:
```python
import jax
import jax.numpy as jnp
from jax import lax
from jax.sharding import PartitionSpec as P

HEADS = 16
PATCH = 1024


def patch_step(carry, pieces, qkv_weight, proj_weight):
    qkv_total, proj_total = carry
    inputs, upstream_gradient = pieces
    width = inputs.shape[1]
    head_dim = width // HEADS
    scale = 1.0 / head_dim**0.5
    values_in = inputs.astype(jnp.float32)
    mean_removed = values_in - jnp.mean(values_in, axis=1, keepdims=True)
    inverse_deviation = lax.rsqrt(
        jnp.mean(mean_removed * mean_removed, axis=1, keepdims=True) + 1e-05
    )
    standardized_input = mean_removed * inverse_deviation
    normalized_rows = standardized_input.astype(jnp.bfloat16)
    qkv = jnp.dot(normalized_rows, qkv_weight, preferred_element_type=jnp.float32).astype(
        jnp.bfloat16
    )
    attended_grad = jnp.einsum(
        "nd,cd->nc", upstream_gradient, proj_weight, preferred_element_type=jnp.float32
    ).astype(jnp.bfloat16)
    per_block = 4
    attended_parts = []
    query_parts = []
    key_parts = []
    value_parts = []
    span = per_block * head_dim
    for block in range(HEADS // per_block):
        low = block * span
        queries = qkv[:, low : low + span].reshape(-1, per_block, head_dim)
        key_rows = qkv[:, width + low : width + low + span].reshape(-1, per_block, head_dim)
        value_rows = qkv[:, 2 * width + low : 2 * width + low + span].reshape(
            -1, per_block, head_dim
        )
        scores = (
            jnp.einsum("qhd,khd->hqk", queries, key_rows, preferred_element_type=jnp.float32)
            * scale
        )
        maxima = jnp.max(scores, axis=2, keepdims=True)
        expon = jnp.exp(scores - maxima)
        probs = (expon / jnp.sum(expon, axis=2, keepdims=True)).astype(jnp.bfloat16)
        attended_parts.append(
            jnp.einsum(
                "hqk,khd->qhd", probs, value_rows, preferred_element_type=jnp.float32
            ).reshape(-1, span)
        )
        grad_rows = attended_grad[:, low : low + span].reshape(-1, per_block, head_dim)
        value_parts.append(
            jnp.einsum(
                "hqk,qhd->khd", probs, grad_rows, preferred_element_type=jnp.float32
            ).reshape(-1, span)
        )
        prob_grad = jnp.einsum(
            "qhd,khd->hqk", grad_rows, value_rows, preferred_element_type=jnp.float32
        )
        prob_f = probs.astype(jnp.float32)
        score_grad = (
            prob_f * (prob_grad - jnp.sum(prob_grad * prob_f, axis=2, keepdims=True)) * scale
        ).astype(jnp.bfloat16)
        query_parts.append(
            jnp.einsum(
                "hqk,khd->qhd", score_grad, key_rows, preferred_element_type=jnp.float32
            ).reshape(-1, span)
        )
        key_parts.append(
            jnp.einsum(
                "hqk,qhd->khd", score_grad, queries, preferred_element_type=jnp.float32
            ).reshape(-1, span)
        )
    attended = jnp.concatenate(attended_parts, axis=1).astype(jnp.bfloat16)
    qkv_cot = jnp.concatenate(query_parts + key_parts + value_parts, axis=1).astype(jnp.bfloat16)
    block_out = (
        values_in + jnp.dot(attended, proj_weight, preferred_element_type=jnp.float32)
    ).astype(jnp.bfloat16)
    proj_total = proj_total + jnp.einsum(
        "nc,nd->cd", attended, upstream_gradient, preferred_element_type=jnp.float32
    )
    qkv_total = qkv_total + jnp.einsum(
        "nc,nd->cd", normalized_rows, qkv_cot, preferred_element_type=jnp.float32
    )
    normalized_gradient = jnp.einsum(
        "ne,ce->nc", qkv_cot, qkv_weight, preferred_element_type=jnp.float32
    )
    gradient_dot_mean = jnp.mean(normalized_gradient, axis=1, keepdims=True)
    mixed_product_mean = jnp.mean(normalized_gradient * standardized_input, axis=1, keepdims=True)
    sorted_gradient = (
        upstream_gradient.astype(jnp.float32)
        + inverse_deviation
        * (normalized_gradient - gradient_dot_mean - standardized_input * mixed_product_mean)
    ).astype(jnp.bfloat16)
    return ((qkv_total, proj_total), (block_out, sorted_gradient))


def rank_within(owners, device_count):
    flags = (owners[:, None] == jnp.arange(device_count, dtype=jnp.int32)[None, :]).astype(
        jnp.int32
    )
    before = jnp.cumsum(flags, axis=0) - flags
    return jnp.sum(before * flags, axis=1)


def on_device(features, zorder_to, hilbert_from, qkv_weight, proj_weight, out_grad):
    row_count, width = features.shape
    row_size = lax.axis_size("row")
    col_size = lax.axis_size("col")
    device_count = row_size * col_size
    capacity = row_count // device_count
    dest_dev = zorder_to // row_count
    send_index = dest_dev * capacity + rank_within(dest_dev, device_count)
    source_dev = hilbert_from // row_count
    by_zorder = jnp.argsort(hilbert_from)
    sorted_rank = rank_within(source_dev[by_zorder], device_count)
    recv_rank = jnp.zeros((row_count,), jnp.int32).at[by_zorder].set(sorted_rank)
    recv_index = source_dev * capacity + recv_rank
    outbound = (
        jnp.zeros((device_count * capacity, width), jnp.bfloat16).at[send_index].set(features)
    )
    arrived = lax.all_to_all(
        outbound.reshape(device_count, capacity, width),
        ("row", "col"),
        split_axis=0,
        concat_axis=0,
        tiled=True,
    )
    ordered = arrived.reshape(device_count * capacity, width)[recv_index]
    patches = row_count // PATCH
    start = (jnp.zeros((width, 3 * width), jnp.float32), jnp.zeros((width, width), jnp.float32))

    def stepper(carry, pieces):
        return patch_step(carry, pieces, qkv_weight, proj_weight)

    totals, results = lax.scan(
        stepper,
        start,
        (ordered.reshape(patches, PATCH, width), out_grad.reshape(patches, PATCH, width)),
    )
    block_out = results[0].reshape(row_count, width)
    sorted_gradient = results[1].reshape(row_count, width)
    qkv_grad, proj_grad = lax.psum((totals[0], totals[1]), ("row", "col"))
    homebound = (
        jnp.zeros((device_count * capacity, width), jnp.bfloat16)
        .at[recv_index]
        .set(sorted_gradient)
    )
    returned = lax.all_to_all(
        homebound.reshape(device_count, capacity, width),
        ("row", "col"),
        split_axis=0,
        concat_axis=0,
        tiled=True,
    )
    feature_grad = returned.reshape(device_count * capacity, width)[send_index]
    return (block_out, feature_grad, qkv_grad, proj_grad)


def solution(mesh):
    in_specs = (
        P(("row", "col"), None),
        P(("row", "col")),
        P(("row", "col")),
        P(),
        P(),
        P(("row", "col"), None),
    )
    out_specs = (P(("row", "col"), None), P(("row", "col"), None), P(), P())
    return jax.shard_map(
        on_device, mesh=mesh, in_specs=in_specs, out_specs=out_specs, check_vma=False
    )
```

profile of v0, /device:TPU:1, one launch (start us, length us, event | category | flops | bytes accessed | tf_op | source)
XLA Modules:
  0.0 521.2 jit_solution(7608040783917497095)
XLA Ops:
  14.6 6.1 %scatter_custom_fusion = bf16[1024,256]{1,0:T(8,128)(2,1)} fusion(s32[1024]{0:T(1024)S(1)} %get-tuple-element.36, bf16[1024,256]{1,0:T(8,128)(2,1)} %param.6, bf16[]{:T(256)} %constant.56.clone.1), kind=kCustom, calls=%fused_computation.120 | custom fusion | bytes 524800 | tf_op jit(solution)/shard_map/scatter | solution.py:123
  20.7 11.5 %all-to-all-start = ((bf16[128,8,256]{2,1,0:T(8,128)(2,1)}), bf16[128,8,256]{2,1,0:T(8,128)(2,1)S(1)}, u32[]{:S(2)}, u32[]{:S(2)}) async-start(bf16[128,8,256]{2,1,0:T(8,128)(2,1)} %bitcast.4), calls=%async_computation | async-start | bytes 1048576 | tf_op jit(solution)/shard_map/all_to_all | solution.py:125
  51.7 8.1 %fusion.134 = f32[4,1024,1024]{1,2,0:T(8,128)} fusion(bf16[1024,4,16]{0,2,1:T(8,128)(2,1)S(1)} %bitcast.166, bf16[1024,4,16]{0,2,1:T(8,128)(2,1)S(1)} %bitcast.158), kind=kOutput, calls=%fused_computation.201 | convolution fusion | flops 134217728 | bytes 17039360 | tf_op jit(solution)/shard_map/while/body/eval_jaxpr/qhd,khd->hqk/dot_general | solution.py:60
  59.8 8.6 %fusion.126 = (f32[4,1024]{1,0:T(4,128)S(1)}, f32[4,1024,1024]{1,2,0:T(8,128)}) fusion(bf16[1024,4,16]{0,2,1:T(8,128)(2,1)S(1)} %bitcast.192, bf16[1024,4,16]{0,2,1:T(8,128)(2,1)S(1)} %bitcast.194), kind=kOutput, calls=%fused_computation.193 | convolution fusion | flops 146801664 | bytes 17055744 | tf_op jit(solution)/shard_map/while/body/eval_jaxpr/sub | solution.py:47
  68.5 9.2 %divide_convert_fusion = bf16[4,1024,1024]{1,2,0:T(8,128)(2,1)} fusion(f32[4,1024,1024]{1,2,0:T(8,128)} %get-tuple-element.60, f32[4,1024]{1,0:T(4,128)S(1)} %get-tuple-element.59), kind=kLoop, calls=%fused_computation.30 | loop fusion | flops 8388608 | bytes 25182208 | tf_op jit(solution)/shard_map/while/body/eval_jaxpr/convert_element_type | solution.py:48
  77.7 20.3 %fusion.56 = bf16[4,16,1024]{2,1,0:T(8,128)(2,1)S(1)} fusion(bf16[1024,4,16]{0,2,1:T(8,128)(2,1)S(1)} %bitcast.195, bf16[4,1024,1024]{1,2,0:T(8,128)(2,1)} %divide_convert_fusion, f32[4,1024,1024]{1,2,0:T(8,128)} %fusion.134), kind=kOutput, calls=%fused_computation.87 | convolution fusion | flops 163648512 | bytes 25427968 | tf_op jit(solution)/shard_map/while/body/eval_jaxpr/hqk,khd->qhd/dot_general | solution.py:68
  98.0 18.0 %fusion.57 = bf16[4,16,1024]{2,1,0:T(8,128)(2,1)S(1)} fusion(bf16[1024,4,16]{0,2,1:T(8,128)(2,1)S(1)} %bitcast.193, bf16[4,1024,1024]{1,2,0:T(8,128)(2,1)} %divide_convert_fusion, f32[4,1024,1024]{1,2,0:T(8,128)} %fusion.134), kind=kOutput, calls=%fused_computation.88 | convolution fusion | flops 163648512 | bytes 25427968 | tf_op jit(solution)/shard_map/while/body/eval_jaxpr/hqk,qhd->khd/dot_general | solution.py:73
  116.0 5.7 %convolution_convert_fusion.2 = bf16[4,16,1024]{2,1,0:T(8,128)(2,1)S(1)} fusion(bf16[1024,4,16]{0,2,1:T(8,128)(2,1)S(1)} %bitcast.167, bf16[4,1024,1024]{1,2,0:T(8,128)(2,1)} %divide_convert_fusion), kind=kOutput, calls=%fused_computation.73 | convolution fusion | flops 134283264 | bytes 8650752 | tf_op jit(solution)/shard_map/while/body/eval_jaxpr/hqk,qhd->khd/dot_general | solution.py:56
  126.9 8.1 %fusion.131 = f32[4,1024,1024]{1,2,0:T(8,128)} fusion(bf16[1024,4,16]{0,2,1:T(8,128)(2,1)S(1)} %bitcast.164, bf16[1024,4,16]{0,2,1:T(8,128)(2,1)S(1)} %bitcast.156), kind=kOutput, calls=%fused_computation.198 | convolution fusion | flops 134217728 | bytes 17039360 | tf_op jit(solution)/shard_map/while/body/eval_jaxpr/qhd,khd->hqk/dot_general | solution.py:60
  135.0 8.6 %fusion.129 = (f32[4,1024]{1,0:T(4,128)S(1)}, f32[4,1024,1024]{1,2,0:T(8,128)}) fusion(bf16[1024,4,16]{0,2,1:T(8,128)(2,1)S(1)} %bitcast.188, bf16[1024,4,16]{0,2,1:T(8,128)(2,1)S(1)} %bitcast.190), kind=kOutput, calls=%fused_computation.196 | convolution fusion | flops 146801664 | bytes 17055744 | tf_op jit(solution)/shard_map/while/body/eval_jaxpr/sub | solution.py:47
  143.6 9.2 %divide_convert_fusion.3 = bf16[4,1024,1024]{1,2,0:T(8,128)(2,1)} fusion(f32[4,1024,1024]{1,2,0:T(8,128)} %get-tuple-element.66, f32[4,1024]{1,0:T(4,128)S(1)} %get-tuple-element.65), kind=kLoop, calls=%fused_computation.36 | loop fusion | flops 8388608 | bytes 25182208 | tf_op jit(solution)/shard_map/while/body/eval_jaxpr/convert_element_type | solution.py:48
  152.8 20.3 %fusion.50 = bf16[4,16,1024]{2,1,0:T(8,128)(2,1)S(1)} fusion(bf16[1024,4,16]{0,2,1:T(8,128)(2,1)S(1)} %bitcast.191, bf16[4,1024,1024]{1,2,0:T(8,128)(2,1)} %divide_convert_fusion.3, f32[4,1024,1024]{1,2,0:T(8,128)} %fusion.131), kind=kOutput, calls=%fused_computation.81 | convolution fusion | flops 163648512 | bytes 25427968 | tf_op jit(solution)/shard_map/while/body/eval_jaxpr/hqk,khd->qhd/dot_general | solution.py:68
  173.1 18.1 %fusion.51 = bf16[4,16,1024]{2,1,0:T(8,128)(2,1)S(1)} fusion(bf16[1024,4,16]{0,2,1:T(8,128)(2,1)S(1)} %bitcast.189, bf16[4,1024,1024]{1,2,0:T(8,128)(2,1)} %divide_convert_fusion.3, f32[4,1024,1024]{1,2,0:T(8,128)} %fusion.131), kind=kOutput, calls=%fused_computation.82 | convolution fusion | flops 163648512 | bytes 25427968 | tf_op jit(solution)/shard_map/while/body/eval_jaxpr/hqk,qhd->khd/dot_general | solution.py:73
  191.2 5.7 %convolution_convert_fusion.5 = bf16[4,16,1024]{2,1,0:T(8,128)(2,1)S(1)} fusion(bf16[1024,4,16]{0,2,1:T(8,128)(2,1)S(1)} %bitcast.165, bf16[4,1024,1024]{1,2,0:T(8,128)(2,1)} %divide_convert_fusion.3), kind=kOutput, calls=%fused_computation.76 | convolution fusion | flops 134283264 | bytes 8650752 | tf_op jit(solution)/shard_map/while/body/eval_jaxpr/hqk,qhd->khd/dot_general | solution.py:56
  202.1 8.1 %fusion.133 = f32[4,1024,1024]{1,2,0:T(8,128)} fusion(bf16[1024,4,16]{0,2,1:T(8,128)(2,1)S(1)} %bitcast.162, bf16[1024,4,16]{0,2,1:T(8,128)(2,1)S(1)} %bitcast.154), kind=kOutput, calls=%fused_computation.200 | convolution fusion | flops 134217728 | bytes 17039360 | tf_op jit(solution)/shard_map/while/body/eval_jaxpr/qhd,khd->hqk/dot_general | solution.py:60
  210.2 8.6 %fusion.127 = (f32[4,1024]{1,0:T(4,128)S(1)}, f32[4,1024,1024]{1,2,0:T(8,128)}) fusion(bf16[1024,4,16]{0,2,1:T(8,128)(2,1)S(1)} %bitcast.184, bf16[1024,4,16]{0,2,1:T(8,128)(2,1)S(1)} %bitcast.186), kind=kOutput, calls=%fused_computation.194 | convolution fusion | flops 146801664 | bytes 17055744 | tf_op jit(solution)/shard_map/while/body/eval_jaxpr/sub | solution.py:47
  218.8 9.2 %divide_convert_fusion.1 = bf16[4,1024,1024]{1,2,0:T(8,128)(2,1)} fusion(f32[4,1024,1024]{1,2,0:T(8,128)} %get-tuple-element.62, f32[4,1024]{1,0:T(4,128)S(1)} %get-tuple-element.61), kind=kLoop, calls=%fused_computation.32 | loop fusion | flops 8388608 | bytes 25182208 | tf_op jit(solution)/shard_map/while/body/eval_jaxpr/convert_element_type | solution.py:48
  228.0 20.7 %fusion.54 = bf16[4,16,1024]{2,1,0:T(8,128)(2,1)S(1)} fusion(bf16[1024,4,16]{0,2,1:T(8,128)(2,1)S(1)} %bitcast.187, bf16[4,1024,1024]{1,2,0:T(8,128)(2,1)} %divide_convert_fusion.1, f32[4,1024,1024]{1,2,0:T(8,128)} %fusion.133), kind=kOutput, calls=%fused_computation.85 | convolution fusion | flops 163648512 | bytes 25427968 | tf_op jit(solution)/shard_map/while/body/eval_jaxpr/hqk,khd->qhd/dot_general | solution.py:68
  248.7 17.9 %fusion.55 = bf16[4,16,1024]{2,1,0:T(8,128)(2,1)S(1)} fusion(bf16[1024,4,16]{0,2,1:T(8,128)(2,1)S(1)} %bitcast.185, bf16[4,1024,1024]{1,2,0:T(8,128)(2,1)} %divide_convert_fusion.1, f32[4,1024,1024]{1,2,0:T(8,128)} %fusion.133), kind=kOutput, calls=%fused_computation.86 | convolution fusion | flops 163648512 | bytes 25427968 | tf_op jit(solution)/shard_map/while/body/eval_jaxpr/hqk,qhd->khd/dot_general | solution.py:73
  266.6 5.7 %convolution_convert_fusion.3 = bf16[4,16,1024]{2,1,0:T(8,128)(2,1)S(1)} fusion(bf16[1024,4,16]{0,2,1:T(8,128)(2,1)S(1)} %bitcast.163, bf16[4,1024,1024]{1,2,0:T(8,128)(2,1)} %divide_convert_fusion.1), kind=kOutput, calls=%fused_computation.74 | convolution fusion | flops 134283264 | bytes 8650752 | tf_op jit(solution)/shard_map/while/body/eval_jaxpr/hqk,qhd->khd/dot_general | solution.py:56
  272.2 5.3 %convolution_convert_fusion.7 = bf16[4,16,1024]{2,1,0:T(8,128)(2,1)} fusion(bf16[1024,4,16]{0,2,1:T(8,128)(2,1)S(1)} %bitcast.155, bf16[4,1024,1024]{1,2,0:T(8,128)(2,1)} %divide_convert_fusion.1), kind=kOutput, calls=%fused_computation.78 | convolution fusion | flops 134283264 | bytes 8650752 | tf_op jit(solution)/shard_map/while/body/eval_jaxpr/hqk,khd->qhd/dot_general | solution.py:50
  277.5 8.1 %fusion.132 = f32[4,1024,1024]{1,2,0:T(8,128)} fusion(bf16[1024,4,16]{0,2,1:T(8,128)(2,1)S(1)} %bitcast.160, bf16[1024,4,16]{0,2,1:T(8,128)(2,1)S(1)} %bitcast.152), kind=kOutput, calls=%fused_computation.199 | convolution fusion | flops 134217728 | bytes 17039360 | tf_op jit(solution)/shard_map/while/body/eval_jaxpr/qhd,khd->hqk/dot_general | solution.py:60
  285.6 8.8 %fusion.128 = (f32[4,1024]{1,0:T(4,128)S(1)}, f32[4,1024,1024]{1,2,0:T(8,128)}) fusion(bf16[1024,4,16]{0,2,1:T(8,128)(2,1)S(1)} %bitcast.180, bf16[1024,4,16]{0,2,1:T(8,128)(2,1)S(1)} %bitcast.182), kind=kOutput, calls=%fused_computation.195 | convolution fusion | flops 146801664 | bytes 17055744 | tf_op jit(solution)/shard_map/while/body/eval_jaxpr/sub | solution.py:47
  294.4 9.2 %divide_convert_fusion.2 = bf16[4,1024,1024]{1,2,0:T(8,128)(2,1)} fusion(f32[4,1024,1024]{1,2,0:T(8,128)} %get-tuple-element.64, f32[4,1024]{1,0:T(4,128)S(1)} %get-tuple-element.63), kind=kLoop, calls=%fused_computation.34 | loop fusion | flops 8388608 | bytes 25182208 | tf_op jit(solution)/shard_map/while/body/eval_jaxpr/convert_element_type | solution.py:48
  303.6 20.3 %fusion.52 = bf16[4,16,1024]{2,1,0:T(8,128)(2,1)S(1)} fusion(bf16[1024,4,16]{0,2,1:T(8,128)(2,1)S(1)} %bitcast.183, bf16[4,1024,1024]{1,2,0:T(8,128)(2,1)} %divide_convert_fusion.2, f32[4,1024,1024]{1,2,0:T(8,128)} %fusion.132), kind=kOutput, calls=%fused_computation.83 | convolution fusion | flops 163648512 | bytes 25427968 | tf_op jit(solution)/shard_map/while/body/eval_jaxpr/hqk,khd->qhd/dot_general | solution.py:68
  323.9 18.1 %fusion.53 = bf16[4,16,1024]{2,1,0:T(8,128)(2,1)S(1)} fusion(bf16[1024,4,16]{0,2,1:T(8,128)(2,1)S(1)} %bitcast.181, bf16[4,1024,1024]{1,2,0:T(8,128)(2,1)} %divide_convert_fusion.2, f32[4,1024,1024]{1,2,0:T(8,128)} %fusion.132), kind=kOutput, calls=%fused_computation.84 | convolution fusion | flops 163648512 | bytes 25427968 | tf_op jit(solution)/shard_map/while/body/eval_jaxpr/hqk,qhd->khd/dot_general | solution.py:73
  342.0 5.7 %convolution_convert_fusion.4 = bf16[4,16,1024]{2,1,0:T(8,128)(2,1)S(1)} fusion(bf16[1024,4,16]{0,2,1:T(8,128)(2,1)S(1)} %bitcast.161, bf16[4,1024,1024]{1,2,0:T(8,128)(2,1)} %divide_convert_fusion.2), kind=kOutput, calls=%fused_computation.75 | convolution fusion | flops 134283264 | bytes 8650752 | tf_op jit(solution)/shard_map/while/body/eval_jaxpr/hqk,qhd->khd/dot_general | solution.py:56
  347.7 5.3 %convolution_convert_fusion.8 = bf16[4,16,1024]{2,1,0:T(8,128)(2,1)} fusion(bf16[1024,4,16]{0,2,1:T(8,128)(2,1)S(1)} %bitcast.153, bf16[4,1024,1024]{1,2,0:T(8,128)(2,1)} %divide_convert_fusion.2), kind=kOutput, calls=%fused_computation.79 | convolution fusion | flops 134283264 | bytes 8650752 | tf_op jit(solution)/shard_map/while/body/eval_jaxpr/hqk,khd->qhd/dot_general | solution.py:50
  358.6 6.2 %scatter_custom_fusion.2 = bf16[1024,256]{1,0:T(8,128)(2,1)} fusion(s32[1024]{0:T(1024)} %get-tuple-element.38, bf16[1024,256]{1,0:T(8,128)(2,1)S(1)} %gather_fusion.1, f32[1024,256]{1,0:T(8,128)S(1)} %copy.48, bf16[1024,256]{1,0:T(8,128)(2,1)S(1)} %copy-done.1, f32[1024]{0:T(1024)S(1)} %broadcast_multiply_fusion, f32[1024]{0:T(1024)S(1)} %broadcast_multiply_fusion.1, ...), kind=kCustom, calls=%fused_computation.95 | custom fusion | flops 2621440 | bytes 2638336 | tf_op jit(solution)/shard_map/scatter | solution.py:150
  364.9 9.5 %all-to-all-start.1 = ((bf16[128,8,256]{2,1,0:T(8,128)(2,1)}), bf16[128,8,256]{2,1,0:T(8,128)(2,1)S(1)}, u32[]{:S(2)}, u32[]{:S(2)}) async-start(bf16[128,8,256]{2,1,0:T(8,128)(2,1)} %bitcast.58), calls=%async_computation.1 | async-start | bytes 1048576 | tf_op jit(solution)/shard_map/all_to_all | solution.py:152
  376.7 12.0 %all-to-all-done.1 = bf16[128,8,256]{2,1,0:T(8,128)(2,1)S(1)} async-done(((bf16[128,8,256]{2,1,0:T(8,128)(2,1)}), bf16[128,8,256]{2,1,0:T(8,128)(2,1)S(1)}, u32[]{:S(2)}, u32[]{:S(2)}) %all-to-all-start.1) | async-done | bytes 524320 | tf_op jit(solution)/shard_map/all_to_all | solution.py:152
  393.7 116.7 %all-reduce.3.cloned.1.call-done = (f32[256,768]{1,0:T(8,128)}, f32[256,256]{1,0:T(8,128)}) async-done(((f32[256,768]{1,0:T(8,128)}, f32[256,256]{1,0:T(8,128)}), (f32[256,768]{1,0:T(8,128)}, f32[256,256]{1,0:T(8,128)})) %all-reduce.3.cloned.1.call-update) | async-done | bytes 1048592 | tf_op jit(solution)/shard_map/psum | solution.py:146
  (65 shorter events, 53.8 us)
Async XLA Ops:
  7.2 43.5 %copy-start = (bf16[256,768]{1,0:T(8,128)(2,1)S(1)}, bf16[256,768]{1,0:T(8,128)(2,1)}, u32[]{:S(2)}) copy-start(bf16[256,768]{1,0:T(8,128)(2,1)} %param.9) | copy-start | bytes 1179652
  20.7 25.4 %all-to-all-start = ((bf16[128,8,256]{2,1,0:T(8,128)(2,1)}), bf16[128,8,256]{2,1,0:T(8,128)(2,1)S(1)}, u32[]{:S(2)}, u32[]{:S(2)}) async-start(bf16[128,8,256]{2,1,0:T(8,128)(2,1)} %bitcast.4), calls=%async_computation | async-start | bytes 1048576 | tf_op jit(solution)/shard_map/all_to_all | solution.py:125
  32.2 478.2 %all-reduce.3.cloned.1.call-start = ((), (), s32[]{:S(2)}) async-start(), calls=%async_computation.2 | async-start | bytes 2097152 | tf_op jit(solution)/shard_map/psum | solution.py:146
  342.0 14.5 %copy-start.1 = (bf16[1024,256]{1,0:T(8,128)(2,1)S(1)}, bf16[1024,256]{1,0:T(8,128)(2,1)}, u32[]{:S(2)}) copy-start(bf16[1024,256]{1,0:T(8,128)(2,1)} %param.11) | copy-start | bytes 1572868
  364.9 23.9 %all-to-all-start.1 = ((bf16[128,8,256]{2,1,0:T(8,128)(2,1)}), bf16[128,8,256]{2,1,0:T(8,128)(2,1)S(1)}, u32[]{:S(2)}, u32[]{:S(2)}) async-start(bf16[128,8,256]{2,1,0:T(8,128)(2,1)} %bitcast.58), calls=%async_computation.1 | async-start | bytes 1048576 | tf_op jit(solution)/shard_map/all_to_all | solution.py:152
Sparse Core Ops, SparseCore 0:
  358.7 151.6 all-reduce.2
where the time goes:
time: 527 us; the launch traced here: 521 us
  matrix products  274 us (52%)
  waiting for transfers between devices  129 us (24%)
  other arithmetic  53.9 us (10%)
  local copies, waits for them, and re-layouts  29.1 us (6%)
  starting transfers between devices  21.1 us (4%)
  between operations  14.6 us (3%)
    psum x1, waiting for transfers between devices, on_device(): qkv_grad, proj_grad = lax.psum((totals[0], totals[1]), ('row', 'col'))  117 us
    dot_general x4, matrix products, patch_step(): jnp.einsum('hqk,khd->qhd', score_grad, key_rows, preferred_element_type=j...  81.6 us
    dot_general x4, matrix products, patch_step(): jnp.einsum('hqk,qhd->khd', score_grad, queries, preferred_element_type=jn...  72 us
    convert_element_type x4, other arithmetic, patch_step(): probs = (expon / jnp.sum(expon, axis=2, keepdims=True)).astype(jnp.bfloat16)  36.8 us
    sub x4, matrix products, patch_step(): expon = jnp.exp(scores - maxima)  34.8 us
    dot_general x4, matrix products, patch_step(): jnp.einsum('qhd,khd->hqk', grad_rows, value_rows, preferred_element_type=...  32.4 us
    dot_general x4, matrix products, patch_step(): jnp.einsum('hqk,qhd->khd', probs, grad_rows, preferred_element_type=jnp.f...  22.7 us
    dot_general x4, matrix products, patch_step(): jnp.einsum('hqk,khd->qhd', probs, value_rows, preferred_element_type=jnp....  21 us
  transfers between devices with their start and end apart: 3, of which 3 were waited for; matrix products, arithmetic and copies ran while one was open for 5% of the time, Pallas kernels for 0%

commit v1 on v0

v1 whole, which is shorter than its diff:
```python
import functools

import jax
import jax.numpy as jnp
from jax import lax
from jax.experimental import pallas as pl
from jax.experimental.pallas import tpu as pltpu
from jax.sharding import PartitionSpec as P

HEADS = 16
HEAD_DIM = 16
PATCH = 1024
C = 256
QB = 512
CHUNK = 32
CHUNKS = PATCH // CHUNK
STRIP = 256
EXP_SCALE = 0.25 * 1.4426950408889634

F32 = jnp.float32
BF16 = jnp.bfloat16


def dot(a, b):
    return jnp.dot(a, b, preferred_element_type=F32)


def dot_nt(a, b):
    return lax.dot_general(a, b, (((1,), (1,)), ((), ())), preferred_element_type=F32)


def normalize(x):
    centered = x - jnp.mean(x, axis=1, keepdims=True)
    rstd = lax.rsqrt(jnp.mean(centered * centered, axis=1, keepdims=True) + 1e-05)
    return centered * rstd, rstd


def transposed(a):
    return a.astype(F32).T.astype(BF16)


MESH = pl.DeviceIdType.MESH
N_ROW = 8
N_COL = 16
DEVICES = N_ROW * N_COL
CHIPS = DEVICES // 2
CAP = PATCH // DEVICES
LANES = 128


def slots(key_row):
    key_col = jnp.broadcast_to(key_row, (LANES, PATCH)).T
    ranks = []
    for block in range(PATCH // LANES):
        keys = key_row[:, block * LANES : (block + 1) * LANES]
        below = jnp.where(key_col < keys, 1.0, 0.0)
        ranks.append(jnp.sum(below, axis=0, keepdims=True))
    return jnp.concatenate(ranks, axis=1)


def scatter_matrix(slot_row):
    position = lax.broadcasted_iota(jnp.int32, (PATCH, PATCH), 0).astype(F32)
    return jnp.where(slot_row == position, 1.0, 0.0).astype(BF16)


def gather_matrix(slot_row):
    slot_col = jnp.broadcast_to(slot_row, (LANES, PATCH)).T
    lane = lax.broadcasted_iota(jnp.int32, (PATCH, LANES), 1)
    blocks = [
        jnp.where(slot_col == (lane + block * LANES).astype(F32), 1.0, 0.0).astype(BF16)
        for block in range(PATCH // LANES)
    ]
    return jnp.concatenate(blocks, axis=1)


def chip_major(point):
    device = point // PATCH
    row, col = device // N_COL, device % N_COL
    return ((row // 2) * N_COL + col) * 2 + row % 2


def send_slots(zorder_ref):
    point = zorder_ref[...]
    return slots((chip_major(point) * PATCH + point % PATCH).astype(F32))


def recv_slots(hilbert_ref):
    local = lax.broadcasted_iota(jnp.int32, (1, PATCH), 1)
    return slots((chip_major(hilbert_ref[...]) * PATCH + local).astype(F32))


def packed(rows):
    rows = rows.reshape(DEVICES, CAP, C)
    pieces = jnp.concatenate([rows[:, :, :LANES], rows[:, :, LANES:]], axis=1).astype(BF16)
    return pieces.reshape(CHIPS, 2, 2 * CAP, LANES)


def unpacked(pieces):
    pieces = pieces.reshape(DEVICES, 2 * CAP, LANES).astype(F32)
    left = pieces[:, :CAP].reshape(PATCH, LANES)
    right = pieces[:, CAP:].reshape(PATCH, LANES)
    return jnp.concatenate([left, right], axis=1).astype(BF16)


def position():
    row, col = lax.axis_index("row"), lax.axis_index("col")
    core = lax.rem(row, 2)
    return core, (row // 2) * N_COL + col, (row + 1 - 2 * core, col)


def chip_after(step):
    core, chip, _ = position()
    other = lax.rem(chip + step, CHIPS)
    return other, ((other // N_COL) * 2 + core, lax.rem(other, N_COL))


def for_chips(act):
    def body(step, _):
        act(*chip_after(step))
        return 0

    lax.fori_loop(1, CHIPS, body, 0)


def greet(barrier):
    _, _, sibling = position()
    pl.semaphore_signal(barrier, inc=1, device_id=sibling, device_id_type=MESH)
    for_chips(
        lambda _, device: pl.semaphore_signal(
            barrier, inc=1, device_id=device, device_id_type=MESH
        )
    )


def pair_copy(out_ref, both_ref, send_sem, recv_sem):
    core, _, sibling = position()
    return pltpu.make_async_remote_copy(
        src_ref=out_ref.at[:, 1 - core],
        dst_ref=both_ref.at[:, core],
        send_sem=send_sem,
        recv_sem=recv_sem,
        device_id=sibling,
        device_id_type=MESH,
    )


def chip_copies(both_ref, in_ref, send_sem, recv_sem):
    _, chip, _ = position()
    for_chips(
        lambda other, device: pltpu.make_async_remote_copy(
            src_ref=both_ref.at[other],
            dst_ref=in_ref.at[chip],
            send_sem=send_sem,
            recv_sem=recv_sem,
            device_id=device,
            device_id_type=MESH,
        ).start()
    )
    in_ref[chip] = both_ref[chip]


def wait_bytes(ref, count, sem):
    view = ref.at[pl.ds(0, count)]
    pltpu.make_async_copy(view, view, sem).wait()


GROUPS = 2
GROUP_HEADS = HEADS // GROUPS
GROUP_ROWS = C // GROUPS


def tiles(section):
    section = section.reshape(GROUP_ROWS // 8, 8, C)
    halves = [section[:, None, :, :LANES], section[:, None, :, LANES:]]
    return jnp.concatenate(halves, axis=1).reshape(CHIPS // 2, 8, LANES)


def untiled(pieces):
    pieces = pieces.reshape(GROUP_ROWS // 8, 2, 8, LANES)
    return jnp.concatenate([pieces[:, 0], pieces[:, 1]], axis=2).reshape(GROUP_ROWS, C)


def block_kernel(
    feat_hbm, zorder_hbm, hilbert_hbm, wqkv_hbm, wp_hbm, og_hbm,
    out_ref, feat_grad_ref, qkvg_ref, projg_ref,
    feat_ref, zorder_ref, hilbert_ref, wqkv_ref, wp_ref, og_ref, oga_ref, x_ref, normed_ref,
    xhat_ref, rstd_ref, k_ref, v_ref, qt_ref, kt_ref, vt_ref, dot_ref,
    p_ref, ds_ref, e_ref, at_ref, dqt_ref, dkt_ref, dvt_ref,
    there_out, there_both, there_in, back_out, back_both, back_in,
    part_ref, half_ref, sum_ref, chunk_in_ref, result_ref, total_ref,
    load_sems, there_sems, back_sems, group_sems,
):
    half_width = C // 2
    core, chip, sibling = position()
    barrier = pltpu.get_barrier_semaphore()
    sources = (zorder_hbm, feat_hbm, hilbert_hbm, og_hbm, wp_hbm, wqkv_hbm)
    targets = (zorder_ref, feat_ref, hilbert_ref, og_ref, wp_ref, wqkv_ref)
    loads = [
        pltpu.make_async_copy(source, target, load_sems.at[i])
        for i, (source, target) in enumerate(zip(sources, targets))
    ]
    for load in loads:
        load.start()
    greet(barrier)
    loads[0].wait()
    scatter = scatter_matrix(send_slots(zorder_ref))
    loads[1].wait()
    there_out[...] = packed(dot(scatter, feat_ref[...]))
    pl.semaphore_wait(barrier, CHIPS)
    pair = pair_copy(there_out, there_both, there_sems.at[0], there_sems.at[1])
    pair.start()
    there_both[:, core] = there_out[:, core]
    pair.wait()
    chip_copies(there_both, there_in, there_sems.at[2], there_sems.at[3])

    for load in loads[2:]:
        load.wait()
    oga_ref[...] = dot(scatter_matrix(recv_slots(hilbert_ref)), og_ref[...]).astype(BF16)
    do_t = dot_nt(wp_ref[...], oga_ref[...]).astype(BF16).astype(F32)
    dot_ref[...] = (do_t * 0.25).astype(BF16).reshape(HEADS, HEAD_DIM, PATCH)
    wqkv_t = transposed(wqkv_ref[...])
    p_ref[1] = jnp.zeros((PATCH, QB), BF16)
    ds_ref[1] = jnp.zeros((PATCH, QB), BF16)
    dkt_ref[0] = jnp.zeros((HEAD_DIM, PATCH), F32)
    dvt_ref[0] = jnp.zeros((HEAD_DIM, PATCH), F32)
    wait_bytes(there_in, CHIPS - 1, there_sems.at[3])

    x = unpacked(there_in[...])
    x_ref[...] = x
    xhat, rstd = normalize(x.astype(F32))
    xhat_ref[...] = xhat
    rstd_ref[...] = rstd
    normed = xhat.astype(BF16)
    normed_ref[...] = normed
    kv = dot(normed, wqkv_ref[:, C:]).astype(BF16)
    for ref, low in ((k_ref, 0), (v_ref, C)):
        ref[0] = kv[:, low : low + half_width]
        ref[1] = kv[:, low + half_width : low + C]
    qkv_t = dot(wqkv_t, transposed(normed)).astype(BF16)
    for ref, part in ((qt_ref, 0), (kt_ref, 1), (vt_ref, 2)):
        ref[...] = qkv_t[part * C : (part + 1) * C].reshape(HEADS, HEAD_DIM, PATCH)

    def group_part(g):
        heads = slice(g * GROUP_HEADS, (g + 1) * GROUP_HEADS)
        for section, ref in enumerate((dqt_ref, dkt_ref, dvt_ref, at_ref)):
            rows = ref[heads].reshape(GROUP_ROWS, PATCH).astype(BF16)
            other = oga_ref if section == 3 else normed_ref
            low = section % 2 * (CHIPS // 2)
            part_ref[g, section // 2, low : low + CHIPS // 2] = tiles(dot(rows, other[...]))

    def group_half(g):
        return pltpu.make_async_remote_copy(
            src_ref=part_ref.at[g, 1 - core],
            dst_ref=half_ref.at[g],
            send_sem=group_sems.at[g, 0],
            recv_sem=group_sems.at[g, 1],
            device_id=sibling,
            device_id_type=MESH,
        )

    def group_scatter(g):
        group_half(g).wait()
        sum_ref[g] = part_ref[g, core] + half_ref[g]
        for_chips(
            lambda other, device: pltpu.make_async_remote_copy(
                src_ref=sum_ref.at[g, other],
                dst_ref=chunk_in_ref.at[g, chip],
                send_sem=group_sems.at[g, 2],
                recv_sem=group_sems.at[g, 3],
                device_id=device,
                device_id_type=MESH,
            ).start()
        )
        chunk_in_ref[g, chip] = sum_ref[g, chip]

    def group_gather(g):
        wait_bytes(chunk_in_ref.at[g], CHIPS - 1, group_sems.at[g, 3])
        result_ref[g] = jnp.sum(chunk_in_ref[g], axis=0)
        for_chips(
            lambda other, device: pltpu.make_async_remote_copy(
                src_ref=result_ref.at[g],
                dst_ref=total_ref.at[g, core, chip],
                send_sem=group_sems.at[g, 4],
                recv_sem=group_sems.at[g, 5],
                device_id=device,
                device_id_type=MESH,
            ).start()
        )
        total_ref[g, core, chip] = result_ref[g]

    def group_final(g):
        return pltpu.make_async_remote_copy(
            src_ref=total_ref.at[g, core],
            dst_ref=total_ref.at[g, core],
            send_sem=group_sems.at[g, 6],
            recv_sem=group_sems.at[g, 7],
            device_id=sibling,
            device_id_type=MESH,
        )

    def group_finish(g):
        wait_bytes(total_ref.at[g, core], CHIPS - 1, group_sems.at[g, 5])
        group_final(g).start()

    def group_close(g):
        group_final(g).wait()
        wait_bytes(sum_ref.at[g], CHIPS - 1, group_sems.at[g, 2])
        wait_bytes(sum_ref.at[g], CHIPS - 1, group_sems.at[g, 4])
        rows = slice(g * GROUP_ROWS, (g + 1) * GROUP_ROWS)
        for section in range(4):
            low = section % 2 * (CHIPS // 2)
            sums = untiled(total_ref[g, section // 2, low : low + CHIPS // 2])
            if section == 3:
                projg_ref[rows, :] = sums
            else:
                low = section * C + g * GROUP_ROWS
                qkvg_ref[:, low : low + GROUP_ROWS] = sums.T

    def query_side(h, block):
        ql = slice(block * QB, (block + 1) * QB)
        dqt_ref[h, :, ql] = dot(kt_ref[h], ds_ref[block]).astype(BF16)

    def value_side(h, block):
        ql = slice(block * QB, (block + 1) * QB)
        dv = dot_nt(dot_ref[h, :, ql], p_ref[block]) * 4.0
        dvt_ref[h] = dvt_ref[h] + dv if block else dv

    def key_side(h, block):
        ql = slice(block * QB, (block + 1) * QB)
        dk = dot_nt(qt_ref[h, :, ql], ds_ref[block])
        dkt_ref[h] = dkt_ref[h] + dk if block else dk

    behind = (query_side, value_side, key_side)

    def block_step(h, block, km, vm, before):
        half = h // 8
        ql = slice(block * QB, (block + 1) * QB)
        qt = qt_ref[pl.ds(half * 8, 8), :, ql].reshape(half_width, QB)
        dot_t = dot_ref[pl.ds(half * 8, 8), :, ql].reshape(half_width, QB)
        tops, sums = [], []
        for j in range(PATCH // STRIP):
            s = dot(km[j * STRIP : (j + 1) * STRIP], qt)
            if j < len(behind):
                behind[j](before, 1 - block)
            for c in range(STRIP // CHUNK):
                part = s[c * CHUNK : (c + 1) * CHUNK].reshape(CHUNK // 8, 8, QB)
                top = jnp.max(part, axis=0)
                e = jnp.exp2((part - top) * EXP_SCALE)
                e_ref[block, j * (STRIP // CHUNK) + c] = e
                tops.append(top)
                sums.append(jnp.sum(e, axis=0))
        peak = functools.reduce(jnp.maximum, tops)
        peak = jnp.max(peak, axis=0, keepdims=True)
        weights = [jnp.exp2((top - peak) * EXP_SCALE) for top in tops]
        total = functools.reduce(jnp.add, [a * w for a, w in zip(sums, weights)])
        inverse = 1.0 / jnp.sum(total, axis=0, keepdims=True)
        for c in range(CHUNKS):
            p = e_ref[block, c] * (weights[c] * inverse)
            p_ref[block, c * CHUNK : (c + 1) * CHUNK] = p.reshape(CHUNK, QB).astype(BF16)
        ot = dot(vt_ref[h], p_ref[block])
        at_ref[h, :, ql] = ot.astype(BF16)
        delta = jnp.sum(ot * dot_ref[h, :, ql].astype(F32), axis=0, keepdims=True)
        for j in range(PATCH // STRIP):
            dp = dot(vm[j * STRIP : (j + 1) * STRIP], dot_t)
            for c in range(STRIP // CHUNK):
                rows = slice(j * STRIP + c * CHUNK, j * STRIP + (c + 1) * CHUNK)
                p = p_ref[block, rows].astype(F32)
                ds = p * (dp[c * CHUNK : (c + 1) * CHUNK] - delta)
                ds_ref[block, rows] = ds.astype(BF16)

    def head_step(h, _):
        half = h // 8
        lane = lax.broadcasted_iota(jnp.int32, (1, half_width), 1) // HEAD_DIM
        mask = (lane == h % 8).astype(F32).astype(BF16)
        km = k_ref[half] * mask
        vm = v_ref[half] * mask
        block_step(h, 0, km, vm, jnp.maximum(h - 1, 0))
        block_step(h, 1, km, vm, h)

        @pl.when(h == GROUP_HEADS)
        def _():
            group_part(0)
            group_half(0).start()

        @pl.when(h == GROUP_HEADS + 2)
        def _():
            group_scatter(0)

        @pl.when(h == GROUP_HEADS + 4)
        def _():
            group_gather(0)

        @pl.when(h == GROUP_HEADS + 6)
        def _():
            group_finish(0)

        return 0

    lax.fori_loop(0, HEADS, head_step, 0)
    for side in behind:
        side(HEADS - 1, 1)

    group_part(1)
    group_half(1).start()
    cot_t = [ref[...].reshape(C, PATCH).astype(BF16) for ref in (dqt_ref, dkt_ref, dvt_ref)]
    ng = dot(wqkv_ref[...], jnp.concatenate(cot_t, axis=0)).T
    xhat = xhat_ref[...]
    ng_mean = jnp.mean(ng, axis=1, keepdims=True)
    mixed = jnp.mean(ng * xhat, axis=1, keepdims=True)
    back_out[...] = packed(
        oga_ref[...].astype(F32) + rstd_ref[...] * (ng - ng_mean - xhat * mixed)
    )
    back = pair_copy(back_out, back_both, back_sems.at[0], back_sems.at[1])
    back.start()
    back_both[:, core] = back_out[:, core]
    group_scatter(1)
    back.wait()
    chip_copies(back_both, back_in, back_sems.at[2], back_sems.at[3])

    at = at_ref[...].reshape(C, PATCH)
    block_out = x_ref[...].astype(F32) + dot(transposed(at), wp_ref[...])
    gather = gather_matrix(recv_slots(hilbert_ref))
    out_ref[...] = dot(gather, block_out.astype(BF16)).astype(BF16)
    group_close(0)
    group_gather(1)
    gather = gather_matrix(send_slots(zorder_ref))
    wait_bytes(back_in, CHIPS - 1, back_sems.at[3])
    feat_grad_ref[...] = dot(gather, unpacked(back_in[...])).astype(BF16)
    group_finish(1)
    wait_bytes(there_in, CHIPS - 1, there_sems.at[2])
    wait_bytes(back_in, CHIPS - 1, back_sems.at[2])
    group_close(1)


def on_device(features, zorder_to, hilbert_from, qkv_weight, proj_weight, out_grad):
    vmem = pl.BlockSpec(memory_space=pltpu.VMEM)
    points = pltpu.VMEM((PATCH, C), BF16)
    index = pltpu.VMEM((1, PATCH), jnp.int32)
    halves = pltpu.VMEM((2, PATCH, C // 2), BF16)
    heads_t = pltpu.VMEM((HEADS, HEAD_DIM, PATCH), BF16)
    heads_f = pltpu.VMEM((HEADS, HEAD_DIM, PATCH), F32)
    queries = pltpu.VMEM((2, PATCH, QB), BF16)
    pieces = pltpu.VMEM((CHIPS, 2, 2 * CAP, LANES), BF16)
    both_cores = pltpu.VMEM((GROUPS, 2, CHIPS, 8, LANES), F32)
    one_core = pltpu.VMEM((GROUPS, CHIPS, 8, LANES), F32)
    return pl.pallas_call(
        block_kernel,
        out_shape=(
            jax.ShapeDtypeStruct((PATCH, C), BF16),
            jax.ShapeDtypeStruct((PATCH, C), BF16),
            jax.ShapeDtypeStruct((C, 3 * C), F32),
            jax.ShapeDtypeStruct((C, C), F32),
        ),
        in_specs=[pl.BlockSpec(memory_space=pl.ANY)] * 6,
        out_specs=(vmem,) * 4,
        scratch_shapes=[
            points, index, index,
            pltpu.VMEM((C, 3 * C), BF16),
            pltpu.VMEM((C, C), BF16),
            points, points, points, points,
            pltpu.VMEM((PATCH, C), F32),
            pltpu.VMEM((PATCH, 1), F32),
            halves, halves, heads_t, heads_t, heads_t, heads_t,
            queries, queries,
            pltpu.VMEM((2, CHUNKS, CHUNK // 8, 8, QB), F32),
            heads_t, heads_t, heads_f, heads_f,
            pieces, pieces, pieces, pieces, pieces, pieces,
            both_cores, one_core, one_core, one_core,
            pltpu.VMEM((GROUPS, 8, LANES), F32),
            both_cores,
            pltpu.SemaphoreType.DMA((6,)),
            pltpu.SemaphoreType.DMA((4,)),
            pltpu.SemaphoreType.DMA((4,)),
            pltpu.SemaphoreType.DMA((GROUPS, 8)),
        ],
        compiler_params=pltpu.CompilerParams(
            collective_id=0, has_side_effects=True, vmem_limit_bytes=60 * 1024 * 1024
        ),
        cost_estimate=pl.CostEstimate(
            flops=28_000_000_000, bytes_accessed=5_000_000, transcendentals=16_777_216
        ),
    )(
        features,
        zorder_to.reshape(1, PATCH),
        hilbert_from.reshape(1, PATCH),
        qkv_weight,
        proj_weight,
        out_grad,
    )


def solution(mesh):
    in_specs = (
        P(("row", "col"), None),
        P(("row", "col")),
        P(("row", "col")),
        P(),
        P(),
        P(("row", "col"), None),
    )
    out_specs = (P(("row", "col"), None), P(("row", "col"), None), P(), P())
    return jax.shard_map(
        on_device, mesh=mesh, in_specs=in_specs, out_specs=out_specs, check_vma=False
    )
```

time: 527 us -> 112 us (0.21); the launches traced: 521 us -> 112 us
  matrix products: 274 us -> 0 us
  waiting for transfers between devices: 129 us -> 0 us
  Pallas kernels: 0 us -> 106 us
  other arithmetic: 53.9 us -> 0 us
  local copies, waits for them, and re-layouts: 29.1 us -> 5.04 us
  starting transfers between devices: 21.1 us -> 0 us
  between operations: 14.6 us -> 0.65 us
    dot_general x26 -> x0, matrix products: 239 us -> none  [the longest x4 81.6 us: patch_step(): jnp.einsum('hqk,khd->qhd', score_grad, key_rows, preferred_element_type=j...]
    psum x1 -> x0, waiting for transfers between devices: 117 us -> none  [on_device(): qkv_grad, proj_grad = lax.psum((totals[0], totals[1]), ('row', 'col'))]
    pallas_call x0 -> x1, Pallas kernels: none -> 106 us  [on_device(): pl.pallas_call(block_kernel, out_shape=(jax.ShapeDtypeStruct((PATCH, C),...]
    convert_element_type x4 -> x0, other arithmetic: 36.8 us -> none  [patch_step(): probs = (expon / jnp.sum(expon, axis=2, keepdims=True)).astype(jnp.bfloat16)]
    sub x4 -> x0, matrix products: 34.8 us -> none  [patch_step(): expon = jnp.exp(scores - maxima)]
    all_to_all x2 -> x0, starting transfers between devices: 21 us -> none  [the longest x1 11.5 us: on_device(): lax.all_to_all(outbound.reshape(device_count, capacity, width), ('row', '...]
    gather x3 -> x0, local copies, waits for them, and re-layouts: 13.4 us -> none  [the longest x1 4.98 us: on_device(): feature_grad = returned.reshape(device_count * capacity, width)[send_index]]
    all_to_all x2 -> x0, waiting for transfers between devices: 12.2 us -> none  [the longest x1 12 us: on_device(): lax.all_to_all(homebound.reshape(device_count, capacity, width), ('row',...]
  transfers between devices with their start and end apart: 3 -> 0, of which waited for: 3 -> 0; matrix products, arithmetic and copies ran while one was open for 5% -> 0% of each run, Pallas kernels for 0% -> 0%
where the time goes in v1:
time: 112 us
  Pallas kernels  106 us (95%)
  local copies, waits for them, and re-layouts  5.04 us (4%)
    pallas_call x1, Pallas kernels, on_device(): pl.pallas_call(block_kernel, out_shape=(jax.ShapeDtypeStruct((PATCH, C),...  106 us
    unnamed x10, local copies, waits for them, and re-layouts  5.04 us

profile of v1, /device:TPU:1, one launch (start us, length us, event | category | flops | bytes accessed | tf_op | source)
XLA Modules:
  0.0 112.0 jit_solution(16530174972208811332)
XLA Ops:
  0.6 106.3 %shard_map.93 = (bf16[1024,256]{1,0:T(8,128)(2,1)}, bf16[1024,256]{1,0:T(8,128)(2,1)}, f32[256,768]{1,0:T(8,128)}, f32[256,256]{1,0:T(8,128)}) custom-call(bf16[1024,256]{1,0:T(8,128)(2,1)} %feat_hbm.1, s32[1,1024]{1,0:T(1,128)} %bitcast.2, s32[1,1024]{1,0:T(1,128)} %bitcast.3, bf16[256,768]{1,0:T(8,128)(2,1)} %wqkv_hbm.1, bf16[256,256]{1,0:T(8,128)(2,1)} %wp_hbm.1, ...), custom_call_target="tpu_custom_call" | custom-call | flops 28000000000 | bytes 5000000 | tf_op jit(solution)/shard_map/pallas_call | solution.py:446
  107.0 0.0 copy-start.1
  107.0 1.9 %copy.14 = bf16[1024,256]{1,0:T(8,128)(2,1)} copy(bf16[1024,256]{1,0:T(8,128)(2,1)} %get-tuple-element.8) | data formatting | bytes 1048576
  108.9 0.0 copy-done.1
  108.9 0.0 copy-start
  108.9 0.8 copy.15
  109.7 0.5 copy-done
  110.2 0.0 copy-start.2
  110.2 0.9 copy.16
  111.1 0.2 copy-done.2
  111.3 0.7 copy.17
Async XLA Ops:
  107.0 1.9 %copy-start.1 = (bf16[1024,256]{1,0:T(8,128)(2,1)S(1)}, bf16[1024,256]{1,0:T(8,128)(2,1)}, u32[]{:S(2)}) copy-start(bf16[1024,256]{1,0:T(8,128)(2,1)} %get-tuple-element.9) | copy-start | bytes 1572868
  108.9 1.3 %copy-start = (f32[256,768]{1,0:T(8,128)S(1)}, f32[256,768]{1,0:T(8,128)}, u32[]{:S(2)}) copy-start(f32[256,768]{1,0:T(8,128)} %get-tuple-element.10) | copy-start | bytes 2359300
  110.2 1.1 copy-start.2

commit v2 on v1

--- a/solution.py
+++ b/solution.py
@@ -48,8 +48,19 @@
 LANES = 128
 
 
+STRIDE = 27
+INVERSE_STRIDE = 19
+PARTS = 4
+PART_DEVICES = DEVICES // PARTS
+PART_ROWS = PATCH // PARTS
+
+
+def as_column(row):
+    return jnp.broadcast_to(row, (LANES, PATCH)).T
+
+
 def slots(key_row):
-    key_col = jnp.broadcast_to(key_row, (LANES, PATCH)).T
+    key_col = as_column(key_row)
     ranks = []
     for block in range(PATCH // LANES):
         keys = key_row[:, block * LANES : (block + 1) * LANES]
@@ -58,48 +69,66 @@
     return jnp.concatenate(ranks, axis=1)
 
 
-def scatter_matrix(slot_row):
-    position = lax.broadcasted_iota(jnp.int32, (PATCH, PATCH), 0).astype(F32)
-    return jnp.where(slot_row == position, 1.0, 0.0).astype(BF16)
-
-
-def gather_matrix(slot_row):
-    slot_col = jnp.broadcast_to(slot_row, (LANES, PATCH)).T
-    lane = lax.broadcasted_iota(jnp.int32, (PATCH, LANES), 1)
+def scatter_rows(slot_row, part):
+    row = lax.broadcasted_iota(jnp.int32, (PART_ROWS, PATCH), 0) + part * PART_ROWS
+    return jnp.where(slot_row == row.astype(F32), 1.0, 0.0).astype(BF16)
+
+
+def gather_columns(slot_col, part):
+    lane = lax.broadcasted_iota(jnp.int32, (PATCH, LANES), 1) + part * PART_ROWS
     blocks = [
-        jnp.where(slot_col == (lane + block * LANES).astype(F32), 1.0, 0.0).astype(BF16)
-        for block in range(PATCH // LANES)
+        jnp.where(slot_col == (lane + low).astype(F32), 1.0, 0.0).astype(BF16)
+        for low in range(0, PART_ROWS, LANES)
     ]
     return jnp.concatenate(blocks, axis=1)
 
 
-def chip_major(point):
-    device = point // PATCH
-    row, col = device // N_COL, device % N_COL
+def linear(row, col):
     return ((row // 2) * N_COL + col) * 2 + row % 2
+
+
+def my_linear():
+    row, col = lax.axis_index("row"), lax.axis_index("col")
+    return ((row // 2) * N_COL + col) * 2 + lax.rem(row, 2)
+
+
+def coordinates(index):
+    chip = index // 2
+    return (chip // N_COL) * 2 + lax.rem(index, 2), lax.rem(chip, N_COL)
+
+
+def relative_slot(offset):
+    return (offset + DEVICES) * INVERSE_STRIDE % DEVICES
 
 
 def send_slots(zorder_ref):
     point = zorder_ref[...]
-    return slots((chip_major(point) * PATCH + point % PATCH).astype(F32))
+    device = point // PATCH
+    there = linear(device // N_COL, device % N_COL)
+    return slots((relative_slot(there - my_linear()) * PATCH + point % PATCH).astype(F32))
 
 
 def recv_slots(hilbert_ref):
+    device = hilbert_ref[...] // PATCH
+    there = linear(device // N_COL, device % N_COL)
     local = lax.broadcasted_iota(jnp.int32, (1, PATCH), 1)
-    return slots((chip_major(hilbert_ref[...]) * PATCH + local).astype(F32))
+    return slots((relative_slot(my_linear() - there) * PATCH + local).astype(F32))
 
 
 def packed(rows):
-    rows = rows.reshape(DEVICES, CAP, C)
-    pieces = jnp.concatenate([rows[:, :, :LANES], rows[:, :, LANES:]], axis=1).astype(BF16)
-    return pieces.reshape(CHIPS, 2, 2 * CAP, LANES)
+    rows = rows.reshape(PART_DEVICES, CAP, C)
+    return jnp.concatenate([rows[:, :, :LANES], rows[:, :, LANES:]], axis=1).astype(BF16)
 
 
 def unpacked(pieces):
-    pieces = pieces.reshape(DEVICES, 2 * CAP, LANES).astype(F32)
-    left = pieces[:, :CAP].reshape(PATCH, LANES)
-    right = pieces[:, CAP:].reshape(PATCH, LANES)
+    pieces = pieces.astype(F32)
+    left = pieces[:, :CAP].reshape(PART_ROWS, LANES)
+    right = pieces[:, CAP:].reshape(PART_ROWS, LANES)
     return jnp.concatenate([left, right], axis=1).astype(BF16)
+
+
+def part_pieces(part):
+    return slice(part * PART_DEVICES, (part + 1) * PART_DEVICES)
 
 
 def position():
@@ -108,55 +137,49 @@
     return core, (row // 2) * N_COL + col, (row + 1 - 2 * core, col)
 
 
-def chip_after(step):
+def for_chips(act):
     core, chip, _ = position()
-    other = lax.rem(chip + step, CHIPS)
-    return other, ((other // N_COL) * 2 + core, lax.rem(other, N_COL))
-
-
-def for_chips(act):
+
     def body(step, _):
-        act(*chip_after(step))
+        other = lax.rem(chip + step * 13, CHIPS)
+        act(other, ((other // N_COL) * 2 + core, lax.rem(other, N_COL)))
         return 0
 
     lax.fori_loop(1, CHIPS, body, 0)
 
 
 def greet(barrier):
-    _, _, sibling = position()
-    pl.semaphore_signal(barrier, inc=1, device_id=sibling, device_id_type=MESH)
-    for_chips(
-        lambda _, device: pl.semaphore_signal(
-            barrier, inc=1, device_id=device, device_id_type=MESH
-        )
-    )
-
-
-def pair_copy(out_ref, both_ref, send_sem, recv_sem):
-    core, _, sibling = position()
-    return pltpu.make_async_remote_copy(
-        src_ref=out_ref.at[:, 1 - core],
-        dst_ref=both_ref.at[:, core],
-        send_sem=send_sem,
-        recv_sem=recv_sem,
-        device_id=sibling,
-        device_id_type=MESH,
-    )
-
-
-def chip_copies(both_ref, in_ref, send_sem, recv_sem):
-    _, chip, _ = position()
-    for_chips(
-        lambda other, device: pltpu.make_async_remote_copy(
-            src_ref=both_ref.at[other],
-            dst_ref=in_ref.at[chip],
+    me = my_linear()
+
+    def body(step, _):
+        device = coordinates(lax.rem(me + step, DEVICES))
+        pl.semaphore_signal(barrier, inc=1, device_id=device, device_id_type=MESH)
+        return 0
+
+    lax.fori_loop(1, DEVICES, body, 0)
+
+
+def send_part(out_ref, in_ref, part, stride, send_sem, recv_sem):
+    me = my_linear()
+
+    def body(step, _):
+        pltpu.make_async_remote_copy(
+            src_ref=out_ref.at[step],
+            dst_ref=in_ref.at[step],
             send_sem=send_sem,
             recv_sem=recv_sem,
-            device_id=device,
+            device_id=coordinates(lax.rem(me + step * stride, DEVICES)),
             device_id_type=MESH,
         ).start()
-    )
-    in_ref[chip] = both_ref[chip]
+        return 0
+
+    lax.fori_loop(max(part * PART_DEVICES, 1), (part + 1) * PART_DEVICES, body, 0)
+    if part == 0:
+        in_ref[0] = out_ref[0]
+
+
+def wait_part(in_ref, part, recv_sem):
+    wait_bytes(in_ref, PART_DEVICES - (part == 0), recv_sem)
 
 
 def wait_bytes(ref, count, sem):
@@ -182,13 +205,14 @@
 
 def block_kernel(
     feat_hbm, zorder_hbm, hilbert_hbm, wqkv_hbm, wp_hbm, og_hbm,
+    out_hbm, feat_grad_hbm, qkvg_hbm, projg_hbm,
     out_ref, feat_grad_ref, qkvg_ref, projg_ref,
     feat_ref, zorder_ref, hilbert_ref, wqkv_ref, wp_ref, og_ref, oga_ref, x_ref, normed_ref,
-    xhat_ref, rstd_ref, k_ref, v_ref, qt_ref, kt_ref, vt_ref, dot_ref,
+    wqkv_t_ref, xhat_ref, rstd_ref, k_ref, v_ref, qt_ref, kt_ref, vt_ref, dot_ref,
     p_ref, ds_ref, e_ref, at_ref, dqt_ref, dkt_ref, dvt_ref,
-    there_out, there_both, there_in, back_out, back_both, back_in,
+    there_out, there_in, back_out, back_in,
     part_ref, half_ref, sum_ref, chunk_in_ref, result_ref, total_ref,
-    load_sems, there_sems, back_sems, group_sems,
+    load_sems, there_sems, back_sems, group_sems, store_sems,
 ):
     half_width = C // 2
     core, chip, sibling = position()
@@ -199,46 +223,61 @@
         pltpu.make_async_copy(source, target, load_sems.at[i])
         for i, (source, target) in enumerate(zip(sources, targets))
     ]
+    stores = [
+        pltpu.make_async_copy(source, target, store_sems.at[i])
+        for i, (source, target) in enumerate((
+            (out_ref, out_hbm),
+            (feat_grad_ref, feat_grad_hbm),
+            (qkvg_ref, qkvg_hbm),
+            (projg_ref, projg_hbm),
+        ))
+    ]
     for load in loads:
         load.start()
     greet(barrier)
     loads[0].wait()
-    scatter = scatter_matrix(send_slots(zorder_ref))
+    there_slots = send_slots(zorder_ref)
     loads[1].wait()
-    there_out[...] = packed(dot(scatter, feat_ref[...]))
-    pl.semaphore_wait(barrier, CHIPS)
-    pair = pair_copy(there_out, there_both, there_sems.at[0], there_sems.at[1])
-    pair.start()
-    there_both[:, core] = there_out[:, core]
-    pair.wait()
-    chip_copies(there_both, there_in, there_sems.at[2], there_sems.at[3])
+    for part in range(PARTS):
+        rows = dot(scatter_rows(there_slots, part), feat_ref[...])
+        there_out[part_pieces(part)] = packed(rows)
+        if part == 0:
+            pl.semaphore_wait(barrier, DEVICES - 1)
+        send_part(
+            there_out, there_in, part, STRIDE, there_sems.at[PARTS], there_sems.at[part]
+        )
 
     for load in loads[2:]:
         load.wait()
-    oga_ref[...] = dot(scatter_matrix(recv_slots(hilbert_ref)), og_ref[...]).astype(BF16)
+    back_slots = recv_slots(hilbert_ref)
+    for part in range(PARTS):
+        rows = slice(part * PART_ROWS, (part + 1) * PART_ROWS)
+        oga_ref[rows] = dot(scatter_rows(back_slots, part), og_ref[...]).astype(BF16)
     do_t = dot_nt(wp_ref[...], oga_ref[...]).astype(BF16).astype(F32)
     dot_ref[...] = (do_t * 0.25).astype(BF16).reshape(HEADS, HEAD_DIM, PATCH)
-    wqkv_t = transposed(wqkv_ref[...])
+    wqkv_t_ref[...] = transposed(wqkv_ref[...])
     p_ref[1] = jnp.zeros((PATCH, QB), BF16)
     ds_ref[1] = jnp.zeros((PATCH, QB), BF16)
     dkt_ref[0] = jnp.zeros((HEAD_DIM, PATCH), F32)
     dvt_ref[0] = jnp.zeros((HEAD_DIM, PATCH), F32)
-    wait_bytes(there_in, CHIPS - 1, there_sems.at[3])
-
-    x = unpacked(there_in[...])
-    x_ref[...] = x
-    xhat, rstd = normalize(x.astype(F32))
-    xhat_ref[...] = xhat
-    rstd_ref[...] = rstd
-    normed = xhat.astype(BF16)
-    normed_ref[...] = normed
-    kv = dot(normed, wqkv_ref[:, C:]).astype(BF16)
-    for ref, low in ((k_ref, 0), (v_ref, C)):
-        ref[0] = kv[:, low : low + half_width]
-        ref[1] = kv[:, low + half_width : low + C]
-    qkv_t = dot(wqkv_t, transposed(normed)).astype(BF16)
-    for ref, part in ((qt_ref, 0), (kt_ref, 1), (vt_ref, 2)):
-        ref[...] = qkv_t[part * C : (part + 1) * C].reshape(HEADS, HEAD_DIM, PATCH)
+
+    for part in range(PARTS):
+        wait_part(there_in, part, there_sems.at[part])
+        rows = slice(part * PART_ROWS, (part + 1) * PART_ROWS)
+        x = unpacked(there_in[part_pieces(part)])
+        x_ref[rows] = x
+        xhat, rstd = normalize(x.astype(F32))
+        xhat_ref[rows] = xhat
+        rstd_ref[rows] = rstd
+        normed = xhat.astype(BF16)
+        normed_ref[rows] = normed
+        kv = dot(normed, wqkv_ref[:, C:]).astype(BF16)
+        for ref, low in ((k_ref, 0), (v_ref, C)):
+            ref[0, rows] = kv[:, low : low + half_width]
+            ref[1, rows] = kv[:, low + half_width : low + C]
+        qkv_t = dot(wqkv_t_ref[...], transposed(normed)).astype(BF16)
+        for ref, low in ((qt_ref, 0), (kt_ref, C), (vt_ref, 2 * C)):
+            ref[:, :, rows] = qkv_t[low : low + C].reshape(HEADS, HEAD_DIM, PART_ROWS)
 
     def group_part(g):
         heads = slice(g * GROUP_HEADS, (g + 1) * GROUP_HEADS)
@@ -330,8 +369,6 @@
         dk = dot_nt(qt_ref[h, :, ql], ds_ref[block])
         dkt_ref[h] = dkt_ref[h] + dk if block else dk
 
-    behind = (query_side, value_side, key_side)
-
     def block_step(h, block, km, vm, before):
         half = h // 8
         ql = slice(block * QB, (block + 1) * QB)
@@ -340,8 +377,8 @@
         tops, sums = [], []
         for j in range(PATCH // STRIP):
             s = dot(km[j * STRIP : (j + 1) * STRIP], qt)
-            if j < len(behind):
-                behind[j](before, 1 - block)
+            if j == 0:
+                query_side(before, 1 - block)
             for c in range(STRIP // CHUNK):
                 part = s[c * CHUNK : (c + 1) * CHUNK].reshape(CHUNK // 8, 8, QB)
                 top = jnp.max(part, axis=0)
@@ -349,6 +386,7 @@
                 e_ref[block, j * (STRIP // CHUNK) + c] = e
                 tops.append(top)
                 sums.append(jnp.sum(e, axis=0))
+        value_side(before, 1 - block)
         peak = functools.reduce(jnp.maximum, tops)
         peak = jnp.max(peak, axis=0, keepdims=True)
         weights = [jnp.exp2((top - peak) * EXP_SCALE) for top in tops]
@@ -358,6 +396,7 @@
             p = e_ref[block, c] * (weights[c] * inverse)
             p_ref[block, c * CHUNK : (c + 1) * CHUNK] = p.reshape(CHUNK, QB).astype(BF16)
         ot = dot(vt_ref[h], p_ref[block])
+        key_side(before, 1 - block)
         at_ref[h, :, ql] = ot.astype(BF16)
         delta = jnp.sum(ot * dot_ref[h, :, ql].astype(F32), axis=0, keepdims=True)
         for j in range(PATCH // STRIP):
@@ -397,81 +436,121 @@
         return 0
 
     lax.fori_loop(0, HEADS, head_step, 0)
-    for side in behind:
-        side(HEADS - 1, 1)
+    query_side(HEADS - 1, 1)
+    value_side(HEADS - 1, 1)
+    key_side(HEADS - 1, 1)
 
     group_part(1)
     group_half(1).start()
     cot_t = [ref[...].reshape(C, PATCH).astype(BF16) for ref in (dqt_ref, dkt_ref, dvt_ref)]
-    ng = dot(wqkv_ref[...], jnp.concatenate(cot_t, axis=0)).T
-    xhat = xhat_ref[...]
-    ng_mean = jnp.mean(ng, axis=1, keepdims=True)
-    mixed = jnp.mean(ng * xhat, axis=1, keepdims=True)
-    back_out[...] = packed(
-        oga_ref[...].astype(F32) + rstd_ref[...] * (ng - ng_mean - xhat * mixed)
-    )
-    back = pair_copy(back_out, back_both, back_sems.at[0], back_sems.at[1])
-    back.start()
-    back_both[:, core] = back_out[:, core]
-    group_scatter(1)
-    back.wait()
-    chip_copies(back_both, back_in, back_sems.at[2], back_sems.at[3])
+    ng_t = dot(wqkv_ref[...], jnp.concatenate(cot_t, axis=0))
+    for part in range(PARTS):
+        rows = slice(part * PART_ROWS, (part + 1) * PART_ROWS)
+        ng = ng_t[:, rows].T
+        xhat = xhat_ref[rows]
+        ng_mean = jnp.mean(ng, axis=1, keepdims=True)
+        mixed = jnp.mean(ng * xhat, axis=1, keepdims=True)
+        back_out[part_pieces(part)] = packed(
+            oga_ref[rows].astype(F32) + rstd_ref[rows] * (ng - ng_mean - xhat * mixed)
+        )
+        send_part(
+            back_out, back_in, part, DEVICES - STRIDE, back_sems.at[PARTS], back_sems.at[part]
+        )
+        if part == 1:
+            group_scatter(1)
 
     at = at_ref[...].reshape(C, PATCH)
     block_out = x_ref[...].astype(F32) + dot(transposed(at), wp_ref[...])
-    gather = gather_matrix(recv_slots(hilbert_ref))
-    out_ref[...] = dot(gather, block_out.astype(BF16)).astype(BF16)
+    block_out = block_out.astype(BF16)
+    slot_col = as_column(recv_slots(hilbert_ref))
+    gather = [gather_columns(slot_col, part) for part in range(PARTS)]
+    out_ref[...] = dot(jnp.concatenate(gather, axis=1), block_out).astype(BF16)
+    stores[0].start()
     group_close(0)
     group_gather(1)
-    gather = gather_matrix(send_slots(zorder_ref))
-    wait_bytes(back_in, CHIPS - 1, back_sems.at[3])
-    feat_grad_ref[...] = dot(gather, unpacked(back_in[...])).astype(BF16)
+    slot_col = as_column(send_slots(zorder_ref))
+    total = jnp.zeros((PATCH, C), F32)
+    for part in range(PARTS):
+        gather = gather_columns(slot_col, part)
+        wait_part(back_in, part, back_sems.at[part])
+        total += dot(gather, unpacked(back_in[part_pieces(part)]))
+    feat_grad_ref[...] = total.astype(BF16)
+    stores[1].start()
     group_finish(1)
-    wait_bytes(there_in, CHIPS - 1, there_sems.at[2])
-    wait_bytes(back_in, CHIPS - 1, back_sems.at[2])
+    wait_bytes(there_in, DEVICES - 1, there_sems.at[PARTS])
+    wait_bytes(back_in, DEVICES - 1, back_sems.at[PARTS])
     group_close(1)
+    stores[2].start()
+    stores[3].start()
+    for store in stores:
+        store.wait()
+
+
+def finish_kernel(*refs):
+    sources, targets, rooms, sems = refs[:4], refs[4:8], refs[8:12], refs[12]
+    ins = [
+        pltpu.make_async_copy(source, room, sems.at[0, i])
+        for i, (source, room) in enumerate(zip(sources, rooms))
+    ]
+    outs = [
+        pltpu.make_async_copy(room, target, sems.at[1, i])
+        for i, (room, target) in enumerate(zip(rooms, targets))
+    ]
+    for copy in ins:
+        copy.start()
+    for copy_in, copy_out in zip(ins, outs):
+        copy_in.wait()
+        copy_out.start()
+    for copy in outs:
+        copy.wait()
 
 
 def on_device(features, zorder_to, hilbert_from, qkv_weight, proj_weight, out_grad):
-    vmem = pl.BlockSpec(memory_space=pltpu.VMEM)
+    anywhere = pl.BlockSpec(memory_space=pl.ANY)
+    out_shape = (
+        jax.ShapeDtypeStruct((PATCH, C), BF16),
+        jax.ShapeDtypeStruct((PATCH, C), BF16),
+        jax.ShapeDtypeStruct((C, 3 * C), F32),
+        jax.ShapeDtypeStruct((C, C), F32),
+    )
     points = pltpu.VMEM((PATCH, C), BF16)
     index = pltpu.VMEM((1, PATCH), jnp.int32)
     halves = pltpu.VMEM((2, PATCH, C // 2), BF16)
     heads_t = pltpu.VMEM((HEADS, HEAD_DIM, PATCH), BF16)
     heads_f = pltpu.VMEM((HEADS, HEAD_DIM, PATCH), F32)
     queries = pltpu.VMEM((2, PATCH, QB), BF16)
-    pieces = pltpu.VMEM((CHIPS, 2, 2 * CAP, LANES), BF16)
+    pieces = pltpu.VMEM((DEVICES, 2 * CAP, LANES), BF16)
     both_cores = pltpu.VMEM((GROUPS, 2, CHIPS, 8, LANES), F32)
     one_core = pltpu.VMEM((GROUPS, CHIPS, 8, LANES), F32)
-    return pl.pallas_call(
+    results = pl.pallas_call(
         block_kernel,
-        out_shape=(
-            jax.ShapeDtypeStruct((PATCH, C), BF16),
-            jax.ShapeDtypeStruct((PATCH, C), BF16),
-            jax.ShapeDtypeStruct((C, 3 * C), F32),
-            jax.ShapeDtypeStruct((C, C), F32),
-        ),
-        in_specs=[pl.BlockSpec(memory_space=pl.ANY)] * 6,
-        out_specs=(vmem,) * 4,
+        out_shape=out_shape,
+        in_specs=[anywhere] * 6,
+        out_specs=(anywhere,) * 4,
         scratch_shapes=[
+            points, points,
+            pltpu.VMEM((C, 3 * C), F32),
+            pltpu.VMEM((C, C), F32),
             points, index, index,
             pltpu.VMEM((C, 3 * C), BF16),
             pltpu.VMEM((C, C), BF16),
             points, points, points, points,
+            pltpu.VMEM((3 * C, C), BF16),
             pltpu.VMEM((PATCH, C), F32),
             pltpu.VMEM((PATCH, 1), F32),
             halves, halves, heads_t, heads_t, heads_t, heads_t,
             queries, queries,
             pltpu.VMEM((2, CHUNKS, CHUNK // 8, 8, QB), F32),
             heads_t, heads_t, heads_f, heads_f,
-            pieces, pieces, pieces, pieces, pieces, pieces,
+            pieces, pieces, pieces, pieces,
             both_cores, one_core, one_core, one_core,
             pltpu.VMEM((GROUPS, 8, LANES), F32),
             both_cores,
             pltpu.SemaphoreType.DMA((6,)),
+            pltpu.SemaphoreType.DMA((PARTS + 1,)),
+            pltpu.SemaphoreType.DMA((PARTS + 1,)),
+            pltpu.SemaphoreType.DMA((GROUPS, 8)),
             pltpu.SemaphoreType.DMA((4,)),
-            pltpu.SemaphoreType.DMA((4,)),
-            pltpu.SemaphoreType.DMA((GROUPS, 8)),
         ],
         compiler_params=pltpu.CompilerParams(
             collective_id=0, has_side_effects=True, vmem_limit_bytes=60 * 1024 * 1024
@@ -487,6 +566,20 @@
         proj_weight,
         out_grad,
     )
+    return pl.pallas_call(
+        finish_kernel,
+        out_shape=out_shape,
+        in_specs=[anywhere] * 4,
+        out_specs=(anywhere,) * 4,
+        scratch_shapes=[
+            points, points,
+            pltpu.VMEM((C, 3 * C), F32),
+            pltpu.VMEM((C, C), F32),
+            pltpu.SemaphoreType.DMA((2, 4)),
+        ],
+        compiler_params=pltpu.CompilerParams(vmem_limit_bytes=60 * 1024 * 1024),
+        cost_estimate=pl.CostEstimate(flops=0, bytes_accessed=4_000_000, transcendentals=0),
+    )(*results)
 
 
 def solution(mesh):

time: 112 us -> 110 us (0.982)
  local copies, waits for them, and re-layouts: 5.04 us -> 0 us
  Pallas kernels: 106 us -> 109 us
    unnamed x10 -> x0, local copies, waits for them, and re-layouts: 5.04 us -> none
    pallas_call x1 -> x2, Pallas kernels: 106 us -> 109 us  [the longest x1 107 us: on_device(): pl.pallas_call(block_kernel, out_shape=out_shape, in_specs=[anywhere] * 6...]
where the time goes in v2:
time: 110 us
  Pallas kernels  109 us (99%)
    pallas_call x1, Pallas kernels, on_device(): pl.pallas_call(block_kernel, out_shape=out_shape, in_specs=[anywhere] * 6...  107 us
    pallas_call x1, Pallas kernels, on_device(): pl.pallas_call(finish_kernel, out_shape=out_shape, in_specs=[anywhere] *...  2.48 us

profile of v2, /device:TPU:1, one launch (start us, length us, event | category | flops | bytes accessed | tf_op | source)
XLA Modules:
  0.0 109.9 jit_solution(15816292389138641049)
XLA Ops:
  0.6 106.7 %shard_map.93 = (bf16[1024,256]{1,0:T(8,128)(2,1)}, bf16[1024,256]{1,0:T(8,128)(2,1)}, f32[256,768]{1,0:T(8,128)}, f32[256,256]{1,0:T(8,128)}) custom-call(bf16[1024,256]{1,0:T(8,128)(2,1)} %feat_hbm.1, s32[1,1024]{1,0:T(1,128)} %bitcast.2, s32[1,1024]{1,0:T(1,128)} %bitcast.3, bf16[256,768]{1,0:T(8,128)(2,1)} %wqkv_hbm.1, bf16[256,256]{1,0:T(8,128)(2,1)} %wp_hbm.1, ...), custom_call_target="tpu_custom_call" | custom-call | flops 28000000000 | bytes 5000000 | tf_op jit(solution)/shard_map/pallas_call | solution.py:525
  107.4 2.5 %shard_map.94 = (bf16[1024,256]{1,0:T(8,128)(2,1)}, bf16[1024,256]{1,0:T(8,128)(2,1)}, f32[256,768]{1,0:T(8,128)}, f32[256,256]{1,0:T(8,128)}) custom-call(bf16[1024,256]{1,0:T(8,128)(2,1)} %get-tuple-element.8.refs_0_, bf16[1024,256]{1,0:T(8,128)(2,1)} %get-tuple-element.9.refs_1_, f32[256,768]{1,0:T(8,128)} %get-tuple-element.10.refs_2_, ...), custom_call_target="tpu_custom_call" | custom-call | bytes 4000000 | tf_op jit(solution)/shard_map/pallas_call | solution.py:569

commit v3 on v2

--- a/solution.py
+++ b/solution.py
@@ -48,10 +48,10 @@
 LANES = 128
 
 
-STRIDE = 27
-INVERSE_STRIDE = 19
+STRIDE = 13
+INVERSE_STRIDE = 5
 PARTS = 4
-PART_DEVICES = DEVICES // PARTS
+PART_CHIPS = CHIPS // PARTS
 PART_ROWS = PATCH // PARTS
 
 
@@ -83,52 +83,45 @@
     return jnp.concatenate(blocks, axis=1)
 
 
-def linear(row, col):
-    return ((row // 2) * N_COL + col) * 2 + row % 2
-
-
-def my_linear():
-    row, col = lax.axis_index("row"), lax.axis_index("col")
-    return ((row // 2) * N_COL + col) * 2 + lax.rem(row, 2)
-
-
-def coordinates(index):
-    chip = index // 2
-    return (chip // N_COL) * 2 + lax.rem(index, 2), lax.rem(chip, N_COL)
-
-
-def relative_slot(offset):
-    return (offset + DEVICES) * INVERSE_STRIDE % DEVICES
+def chip_and_core(point):
+    device = point // PATCH
+    row, col = device // N_COL, device % N_COL
+    return (row // 2) * N_COL + col, row % 2
+
+
+def relative_slot(offset, core):
+    return ((offset + CHIPS) * INVERSE_STRIDE % CHIPS) * 2 + core
 
 
 def send_slots(zorder_ref):
     point = zorder_ref[...]
-    device = point // PATCH
-    there = linear(device // N_COL, device % N_COL)
-    return slots((relative_slot(there - my_linear()) * PATCH + point % PATCH).astype(F32))
+    chip, core = chip_and_core(point)
+    slot = relative_slot(chip - position()[1], core)
+    return slots((slot * PATCH + point % PATCH).astype(F32))
 
 
 def recv_slots(hilbert_ref):
-    device = hilbert_ref[...] // PATCH
-    there = linear(device // N_COL, device % N_COL)
+    chip, core = chip_and_core(hilbert_ref[...])
+    slot = relative_slot(position()[1] - chip, core)
     local = lax.broadcasted_iota(jnp.int32, (1, PATCH), 1)
-    return slots((relative_slot(my_linear() - there) * PATCH + local).astype(F32))
+    return slots((slot * PATCH + local).astype(F32))
 
 
 def packed(rows):
-    rows = rows.reshape(PART_DEVICES, CAP, C)
-    return jnp.concatenate([rows[:, :, :LANES], rows[:, :, LANES:]], axis=1).astype(BF16)
+    rows = rows.reshape(2 * PART_CHIPS, CAP, C)
+    pieces = jnp.concatenate([rows[:, :, :LANES], rows[:, :, LANES:]], axis=1).astype(BF16)
+    return pieces.reshape(PART_CHIPS, 2, 2 * CAP, LANES)
 
 
 def unpacked(pieces):
-    pieces = pieces.astype(F32)
+    pieces = pieces.reshape(2 * PART_CHIPS, 2 * CAP, LANES).astype(F32)
     left = pieces[:, :CAP].reshape(PART_ROWS, LANES)
     right = pieces[:, CAP:].reshape(PART_ROWS, LANES)
     return jnp.concatenate([left, right], axis=1).astype(BF16)
 
 
-def part_pieces(part):
-    return slice(part * PART_DEVICES, (part + 1) * PART_DEVICES)
+def part_chips(part):
+    return slice(part * PART_CHIPS, (part + 1) * PART_CHIPS)
 
 
 def position():
@@ -137,49 +130,73 @@
     return core, (row // 2) * N_COL + col, (row + 1 - 2 * core, col)
 
 
+def chip_device(chip):
+    core, _, _ = position()
+    return (chip // N_COL) * 2 + core, lax.rem(chip, N_COL)
+
+
 def for_chips(act):
-    core, chip, _ = position()
+    _, chip, _ = position()
 
     def body(step, _):
-        other = lax.rem(chip + step * 13, CHIPS)
-        act(other, ((other // N_COL) * 2 + core, lax.rem(other, N_COL)))
+        other = lax.rem(chip + step * STRIDE, CHIPS)
+        act(other, chip_device(other))
         return 0
 
     lax.fori_loop(1, CHIPS, body, 0)
 
 
 def greet(barrier):
-    me = my_linear()
-
-    def body(step, _):
-        device = coordinates(lax.rem(me + step, DEVICES))
-        pl.semaphore_signal(barrier, inc=1, device_id=device, device_id_type=MESH)
-        return 0
-
-    lax.fori_loop(1, DEVICES, body, 0)
-
-
-def send_part(out_ref, in_ref, part, stride, send_sem, recv_sem):
-    me = my_linear()
+    _, _, sibling = position()
+    pl.semaphore_signal(barrier, inc=1, device_id=sibling, device_id_type=MESH)
+    for_chips(
+        lambda _, device: pl.semaphore_signal(
+            barrier, inc=1, device_id=device, device_id_type=MESH
+        )
+    )
+
+
+def pair_copy(out_ref, both_ref, part, sems):
+    core, _, sibling = position()
+    return pltpu.make_async_remote_copy(
+        src_ref=out_ref.at[part_chips(part), 1 - core],
+        dst_ref=both_ref.at[part_chips(part), core],
+        send_sem=sems.at[0, part],
+        recv_sem=sems.at[1, part],
+        device_id=sibling,
+        device_id_type=MESH,
+    )
+
+
+def start_part(rows, out_ref, both_ref, part, sems):
+    core, _, _ = position()
+    out_ref[part_chips(part)] = packed(rows)
+    pair_copy(out_ref, both_ref, part, sems).start()
+    both_ref[part_chips(part), core] = out_ref[part_chips(part), core]
+
+
+def send_part(out_ref, both_ref, in_ref, part, stride, sems):
+    _, chip, _ = position()
+    pair_copy(out_ref, both_ref, part, sems).wait()
 
     def body(step, _):
         pltpu.make_async_remote_copy(
-            src_ref=out_ref.at[step],
+            src_ref=both_ref.at[step],
             dst_ref=in_ref.at[step],
-            send_sem=send_sem,
-            recv_sem=recv_sem,
-            device_id=coordinates(lax.rem(me + step * stride, DEVICES)),
+            send_sem=sems.at[2, part],
+            recv_sem=sems.at[3, part],
+            device_id=chip_device(lax.rem(chip + step * stride, CHIPS)),
             device_id_type=MESH,
         ).start()
         return 0
 
-    lax.fori_loop(max(part * PART_DEVICES, 1), (part + 1) * PART_DEVICES, body, 0)
+    lax.fori_loop(max(part * PART_CHIPS, 1), (part + 1) * PART_CHIPS, body, 0)
     if part == 0:
-        in_ref[0] = out_ref[0]
-
-
-def wait_part(in_ref, part, recv_sem):
-    wait_bytes(in_ref, PART_DEVICES - (part == 0), recv_sem)
+        in_ref[0] = both_ref[0]
+
+
+def wait_part(in_ref, part, sem):
+    wait_bytes(in_ref, PART_CHIPS - (part == 0), sem)
 
 
 def wait_bytes(ref, count, sem):
@@ -188,6 +205,7 @@
 
 
 GROUPS = 2
+SIDE = 8
 GROUP_HEADS = HEADS // GROUPS
 GROUP_ROWS = C // GROUPS
 
@@ -210,9 +228,9 @@
     feat_ref, zorder_ref, hilbert_ref, wqkv_ref, wp_ref, og_ref, oga_ref, x_ref, normed_ref,
     wqkv_t_ref, xhat_ref, rstd_ref, k_ref, v_ref, qt_ref, kt_ref, vt_ref, dot_ref,
     p_ref, ds_ref, e_ref, at_ref, dqt_ref, dkt_ref, dvt_ref,
-    there_out, there_in, back_out, back_in,
-    part_ref, half_ref, sum_ref, chunk_in_ref, result_ref, total_ref,
-    load_sems, there_sems, back_sems, group_sems, store_sems,
+    there_out, there_both, there_in, back_out, back_both, back_in,
+    part_ref, half_ref, sum_ref, chunk_in_ref, result_ref, total_ref, low_out_ref, low_in_ref,
+    load_sems, there_sems, back_sems, group_sems, level_sems, store_sems,
 ):
     half_width = C // 2
     core, chip, sibling = position()
@@ -240,12 +258,12 @@
     loads[1].wait()
     for part in range(PARTS):
         rows = dot(scatter_rows(there_slots, part), feat_ref[...])
-        there_out[part_pieces(part)] = packed(rows)
         if part == 0:
-            pl.semaphore_wait(barrier, DEVICES - 1)
-        send_part(
-            there_out, there_in, part, STRIDE, there_sems.at[PARTS], there_sems.at[part]
-        )
+            pl.semaphore_wait(barrier, CHIPS)
+        start_part(rows, there_out, there_both, part, there_sems)
+        if part:
+            send_part(there_out, there_both, there_in, part - 1, STRIDE, there_sems)
+    send_part(there_out, there_both, there_in, PARTS - 1, STRIDE, there_sems)
 
     for load in loads[2:]:
         load.wait()
@@ -262,9 +280,9 @@
     dvt_ref[0] = jnp.zeros((HEAD_DIM, PATCH), F32)
 
     for part in range(PARTS):
-        wait_part(there_in, part, there_sems.at[part])
+        wait_part(there_in, part, there_sems.at[3, part])
         rows = slice(part * PART_ROWS, (part + 1) * PART_ROWS)
-        x = unpacked(there_in[part_pieces(part)])
+        x = unpacked(there_in[part_chips(part)])
         x_ref[rows] = x
         xhat, rstd = normalize(x.astype(F32))
         xhat_ref[rows] = xhat
@@ -341,10 +359,75 @@
         wait_bytes(total_ref.at[g, core], CHIPS - 1, group_sems.at[g, 5])
         group_final(g).start()
 
+    high, low = chip // SIDE, lax.rem(chip, SIDE)
+
+    def level_copy(src, dst, to, sem):
+        return pltpu.make_async_remote_copy(
+            src_ref=src,
+            dst_ref=dst,
+            send_sem=level_sems.at[0, sem],
+            recv_sem=level_sems.at[1, sem],
+            device_id=chip_device(to),
+            device_id_type=MESH,
+        )
+
+    def others(mine, act):
+        def body(step, _):
+            act(lax.rem(mine + step, SIDE))
+            return 0
+
+        lax.fori_loop(1, SIDE, body, 0)
+
+    def level_wait(direction, sem, rows):
+        view = sum_ref.at[0, pl.ds(0, (SIDE - 1) * rows)]
+        pltpu.make_async_copy(view, view, level_sems.at[direction, sem]).wait()
+
+    def run(index):
+        return pl.ds(index * SIDE, SIDE)
+
+    def scatter_high():
+        group_half(0).wait()
+        sum_ref[0] = part_ref[0, core] + half_ref[0]
+        others(high, lambda to: level_copy(
+            sum_ref.at[0, run(to)], chunk_in_ref.at[0, run(high)], to * SIDE + low, 0
+        ).start())
+        chunk_in_ref[0, run(high)] = sum_ref[0, run(high)]
+
+    def scatter_low():
+        level_wait(1, 0, SIDE)
+        summed = chunk_in_ref[0].reshape(SIDE, SIDE, 8, LANES)
+        low_out_ref[...] = jnp.sum(summed, axis=0)
+        others(low, lambda to: level_copy(
+            low_out_ref.at[to], low_in_ref.at[low], high * SIDE + to, 1
+        ).start())
+        low_in_ref[low] = low_out_ref[low]
+
+    def gather_low():
+        level_wait(1, 1, 1)
+        result_ref[0] = jnp.sum(low_in_ref[...], axis=0)
+        others(low, lambda to: level_copy(
+            result_ref.at[0], total_ref.at[0, core, chip], high * SIDE + to, 2
+        ).start())
+        total_ref[0, core, chip] = result_ref[0]
+
+    def gather_high():
+        level_wait(1, 2, 1)
+        others(high, lambda to: level_copy(
+            total_ref.at[0, core, run(high)], total_ref.at[0, core, run(high)], to * SIDE + low, 3
+        ).start())
+
+    def gather_done():
+        level_wait(1, 3, SIDE)
+        group_final(0).start()
+
     def group_close(g):
         group_final(g).wait()
-        wait_bytes(sum_ref.at[g], CHIPS - 1, group_sems.at[g, 2])
-        wait_bytes(sum_ref.at[g], CHIPS - 1, group_sems.at[g, 4])
+        if g == 0:
+            for sem, rows in enumerate((SIDE, 1, 1, SIDE)):
+                level_wait(0, sem, rows)
+        else:
+            wait_bytes(sum_ref.at[g], CHIPS - 1, group_sems.at[g, 2])
+            wait_bytes(sum_ref.at[g], CHIPS - 1, group_sems.at[g, 4])
         rows = slice(g * GROUP_ROWS, (g + 1) * GROUP_ROWS)
         for section in range(4):
             low = section % 2 * (CHIPS // 2)
@@ -421,17 +504,10 @@
             group_part(0)
             group_half(0).start()
 
-        @pl.when(h == GROUP_HEADS + 2)
-        def _():
-            group_scatter(0)
-
-        @pl.when(h == GROUP_HEADS + 4)
-        def _():
-            group_gather(0)
-
-        @pl.when(h == GROUP_HEADS + 6)
-        def _():
-            group_finish(0)
+        for step, act in enumerate(
+            (scatter_high, scatter_low, gather_low, gather_high, gather_done), 1
+        ):
+            pl.when(h == GROUP_HEADS + step)(act)
 
         return 0
 
@@ -450,14 +526,13 @@
         xhat = xhat_ref[rows]
         ng_mean = jnp.mean(ng, axis=1, keepdims=True)
         mixed = jnp.mean(ng * xhat, axis=1, keepdims=True)
-        back_out[part_pieces(part)] = packed(
-            oga_ref[rows].astype(F32) + rstd_ref[rows] * (ng - ng_mean - xhat * mixed)
-        )
-        send_part(
-            back_out, back_in, part, DEVICES - STRIDE, back_sems.at[PARTS], back_sems.at[part]
-        )
+        grad = oga_ref[rows].astype(F32) + rstd_ref[rows] * (ng - ng_mean - xhat * mixed)
+        start_part(grad, back_out, back_both, part, back_sems)
         if part == 1:
             group_scatter(1)
+        if part:
+            send_part(back_out, back_both, back_in, part - 1, CHIPS - STRIDE, back_sems)
+    send_part(back_out, back_both, back_in, PARTS - 1, CHIPS - STRIDE, back_sems)
 
     at = at_ref[...].reshape(C, PATCH)
     block_out = x_ref[...].astype(F32) + dot(transposed(at), wp_ref[...])
@@ -472,13 +547,14 @@
     total = jnp.zeros((PATCH, C), F32)
     for part in range(PARTS):
         gather = gather_columns(slot_col, part)
-        wait_part(back_in, part, back_sems.at[part])
-        total += dot(gather, unpacked(back_in[part_pieces(part)]))
+        wait_part(back_in, part, back_sems.at[3, part])
+        total += dot(gather, unpacked(back_in[part_chips(part)]))
     feat_grad_ref[...] = total.astype(BF16)
     stores[1].start()
     group_finish(1)
-    wait_bytes(there_in, DEVICES - 1, there_sems.at[PARTS])
-    wait_bytes(back_in, DEVICES - 1, back_sems.at[PARTS])
+    for part in range(PARTS):
+        wait_part(there_in, part, there_sems.at[2, part])
+        wait_part(back_in, part, back_sems.at[2, part])
     group_close(1)
     stores[2].start()
     stores[3].start()
@@ -519,7 +595,7 @@
     heads_t = pltpu.VMEM((HEADS, HEAD_DIM, PATCH), BF16)
     heads_f = pltpu.VMEM((HEADS, HEAD_DIM, PATCH), F32)
     queries = pltpu.VMEM((2, PATCH, QB), BF16)
-    pieces = pltpu.VMEM((DEVICES, 2 * CAP, LANES), BF16)
+    pieces = pltpu.VMEM((CHIPS, 2, 2 * CAP, LANES), BF16)
     both_cores = pltpu.VMEM((GROUPS, 2, CHIPS, 8, LANES), F32)
     one_core = pltpu.VMEM((GROUPS, CHIPS, 8, LANES), F32)
     results = pl.pallas_call(
@@ -542,14 +618,17 @@
             queries, queries,
             pltpu.VMEM((2, CHUNKS, CHUNK // 8, 8, QB), F32),
             heads_t, heads_t, heads_f, heads_f,
-            pieces, pieces, pieces, pieces,
+            pieces, pieces, pieces, pieces, pieces, pieces,
             both_cores, one_core, one_core, one_core,
             pltpu.VMEM((GROUPS, 8, LANES), F32),
             both_cores,
+            pltpu.VMEM((SIDE, 8, LANES), F32),
+            pltpu.VMEM((SIDE, 8, LANES), F32),
             pltpu.SemaphoreType.DMA((6,)),
-            pltpu.SemaphoreType.DMA((PARTS + 1,)),
-            pltpu.SemaphoreType.DMA((PARTS + 1,)),
+            pltpu.SemaphoreType.DMA((4, PARTS)),
+            pltpu.SemaphoreType.DMA((4, PARTS)),
             pltpu.SemaphoreType.DMA((GROUPS, 8)),
+            pltpu.SemaphoreType.DMA((2, 4)),
             pltpu.SemaphoreType.DMA((4,)),
         ],
         compiler_params=pltpu.CompilerParams(

time: 110 us -> 111 us (level)
  no operation moved by 1% of the time
where the time goes in v3:
time: 111 us
  Pallas kernels  110 us (99%)
    pallas_call x1, Pallas kernels, on_device(): pl.pallas_call(block_kernel, out_shape=out_shape, in_specs=[anywhere] * 6...  108 us
    pallas_call x1, Pallas kernels, on_device(): pl.pallas_call(finish_kernel, out_shape=out_shape, in_specs=[anywhere] *...  2.48 us

profile of v3, /device:TPU:1, one launch (start us, length us, event | category | flops | bytes accessed | tf_op | source)
XLA Modules:
  0.0 110.7 jit_solution(10715998589719160291)
XLA Ops:
  0.6 107.6 %shard_map.93 = (bf16[1024,256]{1,0:T(8,128)(2,1)}, bf16[1024,256]{1,0:T(8,128)(2,1)}, f32[256,768]{1,0:T(8,128)}, f32[256,256]{1,0:T(8,128)}) custom-call(bf16[1024,256]{1,0:T(8,128)(2,1)} %feat_hbm.1, s32[1,1024]{1,0:T(1,128)} %bitcast.2, s32[1,1024]{1,0:T(1,128)} %bitcast.3, bf16[256,768]{1,0:T(8,128)(2,1)} %wqkv_hbm.1, bf16[256,256]{1,0:T(8,128)(2,1)} %wp_hbm.1, ...), custom_call_target="tpu_custom_call" | custom-call | flops 28000000000 | bytes 5000000 | tf_op jit(solution)/shard_map/pallas_call | solution.py:601
  108.2 2.5 %shard_map.94 = (bf16[1024,256]{1,0:T(8,128)(2,1)}, bf16[1024,256]{1,0:T(8,128)(2,1)}, f32[256,768]{1,0:T(8,128)}, f32[256,256]{1,0:T(8,128)}) custom-call(bf16[1024,256]{1,0:T(8,128)(2,1)} %get-tuple-element.8.refs_0_, bf16[1024,256]{1,0:T(8,128)(2,1)} %get-tuple-element.9.refs_1_, f32[256,768]{1,0:T(8,128)} %get-tuple-element.10.refs_2_, ...), custom_call_target="tpu_custom_call" | custom-call | bytes 4000000 | tf_op jit(solution)/shard_map/pallas_call | solution.py:648

commit v4 on v3

--- a/solution.py
+++ b/solution.py
@@ -12,7 +12,7 @@
 PATCH = 1024
 C = 256
 QB = 512
-CHUNK = 32
+CHUNK = 64
 CHUNKS = PATCH // CHUNK
 STRIP = 256
 EXP_SCALE = 0.25 * 1.4426950408889634
@@ -299,11 +299,16 @@
 
     def group_part(g):
         heads = slice(g * GROUP_HEADS, (g + 1) * GROUP_HEADS)
-        for section, ref in enumerate((dqt_ref, dkt_ref, dvt_ref, at_ref)):
-            rows = ref[heads].reshape(GROUP_ROWS, PATCH).astype(BF16)
-            other = oga_ref if section == 3 else normed_ref
+
+        def rows(ref):
+            return ref[heads].reshape(GROUP_ROWS, PATCH).astype(BF16)
+
+        cot = jnp.concatenate([rows(ref) for ref in (dqt_ref, dkt_ref, dvt_ref)], axis=0)
+        sums = dot(cot, normed_ref[...])
+        sums = [sums[i * GROUP_ROWS : (i + 1) * GROUP_ROWS] for i in range(3)]
+        for section, value in enumerate(sums + [dot(rows(at_ref), oga_ref[...])]):
             low = section % 2 * (CHIPS // 2)
-            part_ref[g, section // 2, low : low + CHIPS // 2] = tiles(dot(rows, other[...]))
+            part_ref[g, section // 2, low : low + CHIPS // 2] = tiles(value)
 
     def group_half(g):
         return pltpu.make_async_remote_copy(
@@ -516,8 +521,6 @@
     value_side(HEADS - 1, 1)
     key_side(HEADS - 1, 1)
 
-    group_part(1)
-    group_half(1).start()
     cot_t = [ref[...].reshape(C, PATCH).astype(BF16) for ref in (dqt_ref, dkt_ref, dvt_ref)]
     ng_t = dot(wqkv_ref[...], jnp.concatenate(cot_t, axis=0))
     for part in range(PARTS):
@@ -528,15 +531,16 @@
         mixed = jnp.mean(ng * xhat, axis=1, keepdims=True)
         grad = oga_ref[rows].astype(F32) + rstd_ref[rows] * (ng - ng_mean - xhat * mixed)
         start_part(grad, back_out, back_both, part, back_sems)
-        if part == 1:
-            group_scatter(1)
         if part:
             send_part(back_out, back_both, back_in, part - 1, CHIPS - STRIDE, back_sems)
     send_part(back_out, back_both, back_in, PARTS - 1, CHIPS - STRIDE, back_sems)
+    group_part(1)
+    group_half(1).start()
 
     at = at_ref[...].reshape(C, PATCH)
     block_out = x_ref[...].astype(F32) + dot(transposed(at), wp_ref[...])
     block_out = block_out.astype(BF16)
+    group_scatter(1)
     slot_col = as_column(recv_slots(hilbert_ref))
     gather = [gather_columns(slot_col, part) for part in range(PARTS)]
     out_ref[...] = dot(jnp.concatenate(gather, axis=1), block_out).astype(BF16)

time: 111 us -> 109 us (0.982)
  Pallas kernels: 110 us -> 108 us
    pallas_call x1, Pallas kernels: 108 us -> 105 us  [on_device(): pl.pallas_call(block_kernel, out_shape=out_shape, in_specs=[anywhere] * 6...]
where the time goes in v4:
time: 109 us
  Pallas kernels  108 us (99%)
    pallas_call x1, Pallas kernels, on_device(): pl.pallas_call(block_kernel, out_shape=out_shape, in_specs=[anywhere] * 6...  105 us
    pallas_call x1, Pallas kernels, on_device(): pl.pallas_call(finish_kernel, out_shape=out_shape, in_specs=[anywhere] *...  2.48 us

profile of v4, /device:TPU:1, one launch (start us, length us, event | category | flops | bytes accessed | tf_op | source)
XLA Modules:
  0.0 108.6 jit_solution(18173540331201001074)
XLA Ops:
  0.6 105.5 %shard_map.93 = (bf16[1024,256]{1,0:T(8,128)(2,1)}, bf16[1024,256]{1,0:T(8,128)(2,1)}, f32[256,768]{1,0:T(8,128)}, f32[256,256]{1,0:T(8,128)}) custom-call(bf16[1024,256]{1,0:T(8,128)(2,1)} %feat_hbm.1, s32[1,1024]{1,0:T(1,128)} %bitcast.2, s32[1,1024]{1,0:T(1,128)} %bitcast.3, bf16[256,768]{1,0:T(8,128)(2,1)} %wqkv_hbm.1, bf16[256,256]{1,0:T(8,128)(2,1)} %wp_hbm.1, ...), custom_call_target="tpu_custom_call" | custom-call | flops 28000000000 | bytes 5000000 | tf_op jit(solution)/shard_map/pallas_call | solution.py:605
  106.1 2.5 %shard_map.94 = (bf16[1024,256]{1,0:T(8,128)(2,1)}, bf16[1024,256]{1,0:T(8,128)(2,1)}, f32[256,768]{1,0:T(8,128)}, f32[256,256]{1,0:T(8,128)}) custom-call(bf16[1024,256]{1,0:T(8,128)(2,1)} %get-tuple-element.8.refs_0_, bf16[1024,256]{1,0:T(8,128)(2,1)} %get-tuple-element.9.refs_1_, f32[256,768]{1,0:T(8,128)} %get-tuple-element.10.refs_2_, ...), custom_call_target="tpu_custom_call" | custom-call | bytes 4000000 | tf_op jit(solution)/shard_map/pallas_call | solution.py:652

commit v5 on v4

--- a/solution.py
+++ b/solution.py
@@ -48,8 +48,8 @@
 LANES = 128
 
 
-STRIDE = 13
-INVERSE_STRIDE = 5
+STRIDE = 1
+INVERSE_STRIDE = 1
 PARTS = 4
 PART_CHIPS = CHIPS // PARTS
 PART_ROWS = PATCH // PARTS
@@ -204,21 +204,31 @@
     pltpu.make_async_copy(view, view, sem).wait()
 
 
-GROUPS = 2
 SIDE = 8
-GROUP_HEADS = HEADS // GROUPS
-GROUP_ROWS = C // GROUPS
+GROUPS = 3
+FIRST_HEAD = (0, 8, 13, HEADS)
+OWNER_STRIDE = 13
+OWNER_INVERSE = 5
+
+
+def group_heads(g):
+    return FIRST_HEAD[g + 1] - FIRST_HEAD[g]
+
+
+def group_tiles(g):
+    return 8 * group_heads(g)
 
 
 def tiles(section):
-    section = section.reshape(GROUP_ROWS // 8, 8, C)
+    rows = section.shape[0]
+    section = section.reshape(rows // 8, 8, C)
     halves = [section[:, None, :, :LANES], section[:, None, :, LANES:]]
-    return jnp.concatenate(halves, axis=1).reshape(CHIPS // 2, 8, LANES)
+    return jnp.concatenate(halves, axis=1).reshape(rows // 4, 8, LANES)
 
 
 def untiled(pieces):
-    pieces = pieces.reshape(GROUP_ROWS // 8, 2, 8, LANES)
-    return jnp.concatenate([pieces[:, 0], pieces[:, 1]], axis=2).reshape(GROUP_ROWS, C)
+    pieces = pieces.reshape(-1, 2, 8, LANES)
+    return jnp.concatenate([pieces[:, 0], pieces[:, 1]], axis=2).reshape(-1, C)
 
 
 def block_kernel(
@@ -298,62 +308,87 @@
             ref[:, :, rows] = qkv_t[low : low + C].reshape(HEADS, HEAD_DIM, PART_ROWS)
 
     def group_part(g):
-        heads = slice(g * GROUP_HEADS, (g + 1) * GROUP_HEADS)
+        heads = slice(FIRST_HEAD[g], FIRST_HEAD[g + 1])
+        count = group_heads(g) * HEAD_DIM
 
         def rows(ref):
-            return ref[heads].reshape(GROUP_ROWS, PATCH).astype(BF16)
+            return ref[heads].reshape(count, PATCH).astype(BF16)
 
         cot = jnp.concatenate([rows(ref) for ref in (dqt_ref, dkt_ref, dvt_ref)], axis=0)
         sums = dot(cot, normed_ref[...])
-        sums = [sums[i * GROUP_ROWS : (i + 1) * GROUP_ROWS] for i in range(3)]
+        sums = [sums[i * count : (i + 1) * count] for i in range(3)]
+        half = group_tiles(g) // 2
         for section, value in enumerate(sums + [dot(rows(at_ref), oga_ref[...])]):
-            low = section % 2 * (CHIPS // 2)
-            part_ref[g, section // 2, low : low + CHIPS // 2] = tiles(value)
+            low = section % 2 * half
+            part_ref[g, section // 2, low : low + half] = tiles(value)
+        group_half(g).start()
 
     def group_half(g):
+        count = pl.ds(0, group_tiles(g))
         return pltpu.make_async_remote_copy(
-            src_ref=part_ref.at[g, 1 - core],
-            dst_ref=half_ref.at[g],
+            src_ref=part_ref.at[g, 1 - core, count],
+            dst_ref=half_ref.at[g, count],
             send_sem=group_sems.at[g, 0],
             recv_sem=group_sems.at[g, 1],
             device_id=sibling,
             device_id_type=MESH,
         )
 
+    my_tile = lax.rem(chip * OWNER_INVERSE, CHIPS)
+
+    def by_owner(g, act):
+        pl.when(my_tile < group_tiles(g))(lambda: act(True))
+        pl.when(my_tile >= group_tiles(g))(lambda: act(False))
+
     def group_scatter(g):
         group_half(g).wait()
-        sum_ref[g] = part_ref[g, core] + half_ref[g]
-        for_chips(
-            lambda other, device: pltpu.make_async_remote_copy(
-                src_ref=sum_ref.at[g, other],
-                dst_ref=chunk_in_ref.at[g, chip],
-                send_sem=group_sems.at[g, 2],
-                recv_sem=group_sems.at[g, 3],
-                device_id=device,
-                device_id_type=MESH,
-            ).start()
-        )
-        chunk_in_ref[g, chip] = sum_ref[g, chip]
+        count = group_tiles(g)
+        sum_ref[g, :count] = part_ref[g, core, :count] + half_ref[g, :count]
+
+        def body(tile, _):
+            owner = lax.rem(tile * OWNER_STRIDE, CHIPS)
+
+            @pl.when(owner != chip)
+            def _():
+                pltpu.make_async_remote_copy(
+                    src_ref=sum_ref.at[g, tile],
+                    dst_ref=chunk_in_ref.at[g, chip],
+                    send_sem=group_sems.at[g, 2],
+                    recv_sem=group_sems.at[g, 3],
+                    device_id=chip_device(owner),
+                    device_id_type=MESH,
+                ).start()
+
+            return 0
+
+        lax.fori_loop(0, count, body, 0)
+
+        @pl.when(my_tile < count)
+        def _():
+            chunk_in_ref[g, chip] = sum_ref[g, my_tile]
 
     def group_gather(g):
-        wait_bytes(chunk_in_ref.at[g], CHIPS - 1, group_sems.at[g, 3])
-        result_ref[g] = jnp.sum(chunk_in_ref[g], axis=0)
-        for_chips(
-            lambda other, device: pltpu.make_async_remote_copy(
-                src_ref=result_ref.at[g],
-                dst_ref=total_ref.at[g, core, chip],
-                send_sem=group_sems.at[g, 4],
-                recv_sem=group_sems.at[g, 5],
-                device_id=device,
-                device_id_type=MESH,
-            ).start()
-        )
-        total_ref[g, core, chip] = result_ref[g]
+        @pl.when(my_tile < group_tiles(g))
+        def _():
+            wait_bytes(chunk_in_ref.at[g], CHIPS - 1, group_sems.at[g, 3])
+            result_ref[g] = jnp.sum(chunk_in_ref[g], axis=0)
+            for_chips(
+                lambda other, device: pltpu.make_async_remote_copy(
+                    src_ref=result_ref.at[g],
+                    dst_ref=total_ref.at[g, core, my_tile],
+                    send_sem=group_sems.at[g, 4],
+                    recv_sem=group_sems.at[g, 5],
+                    device_id=device,
+                    device_id_type=MESH,
+                ).start()
+            )
+            total_ref[g, core, my_tile] = result_ref[g]
 
     def group_final(g):
+        count = pl.ds(0, group_tiles(g))
         return pltpu.make_async_remote_copy(
-            src_ref=total_ref.at[g, core],
-            dst_ref=total_ref.at[g, core],
+            src_ref=total_ref.at[g, core, count],
+            dst_ref=total_ref.at[g, core, count],
             send_sem=group_sems.at[g, 6],
             recv_sem=group_sems.at[g, 7],
             device_id=sibling,
@@ -361,7 +396,10 @@
         )
 
     def group_finish(g):
-        wait_bytes(total_ref.at[g, core], CHIPS - 1, group_sems.at[g, 5])
+        def arrived(owner):
+            wait_bytes(total_ref.at[g, core], group_tiles(g) - owner, group_sems.at[g, 5])
+
+        by_owner(g, arrived)
         group_final(g).start()
 
     high, low = chip // SIDE, lax.rem(chip, SIDE)
@@ -430,18 +468,22 @@
         if g == 0:
             for sem, rows in enumerate((SIDE, 1, 1, SIDE)):
                 level_wait(0, sem, rows)
-        else:
-            wait_bytes(sum_ref.at[g], CHIPS - 1, group_sems.at[g, 2])
-            wait_bytes(sum_ref.at[g], CHIPS - 1, group_sems.at[g, 4])
-        rows = slice(g * GROUP_ROWS, (g + 1) * GROUP_ROWS)
-        for section in range(4):
-            low = section % 2 * (CHIPS // 2)
-            sums = untiled(total_ref[g, section // 2, low : low + CHIPS // 2])
-            if section == 3:
-                projg_ref[rows, :] = sums
-            else:
-                low = section * C + g * GROUP_ROWS
-                qkvg_ref[:, low : low + GROUP_ROWS] = sums.T
+            return
+
+        def sent(owner):
+            wait_bytes(sum_ref.at[g], group_tiles(g) - owner, group_sems.at[g, 2])
+            if owner:
+                wait_bytes(sum_ref.at[g], CHIPS - 1, group_sems.at[g, 4])
+
+        by_owner(g, sent)
+
+    def assemble(section):
+        rows = []
+        for g in range(GROUPS):
+            half = group_tiles(g) // 2
+            low = section % 2 * half
+            rows.append(untiled(total_ref[g, section // 2, low : low + half]))
+        return jnp.concatenate(rows, axis=0)
 
     def query_side(h, block):
         ql = slice(block * QB, (block + 1) * QB)
@@ -495,6 +537,10 @@
                 ds = p * (dp[c * CHUNK : (c + 1) * CHUNK] - delta)
                 ds_ref[block, rows] = ds.astype(BF16)
 
+    def after_scatter():
+        gather_done()
+        group_scatter(1)
+
     def head_step(h, _):
         half = h // 8
         lane = lax.broadcasted_iota(jnp.int32, (1, half_width), 1) // HEAD_DIM
@@ -504,15 +550,18 @@
         block_step(h, 0, km, vm, jnp.maximum(h - 1, 0))
         block_step(h, 1, km, vm, h)
 
-        @pl.when(h == GROUP_HEADS)
-        def _():
-            group_part(0)
-            group_half(0).start()
-
-        for step, act in enumerate(
-            (scatter_high, scatter_low, gather_low, gather_high, gather_done), 1
-        ):
-            pl.when(h == GROUP_HEADS + step)(act)
+        steps = {
+            FIRST_HEAD[1]: lambda: group_part(0),
+            FIRST_HEAD[1] + 1: scatter_high,
+            FIRST_HEAD[1] + 2: scatter_low,
+            FIRST_HEAD[1] + 3: gather_low,
+            FIRST_HEAD[1] + 4: gather_high,
+            FIRST_HEAD[2]: lambda: group_part(1),
+            FIRST_HEAD[2] + 1: after_scatter,
+            FIRST_HEAD[2] + 2: lambda: group_gather(1),
+        }
+        for head, act in steps.items():
+            pl.when(h == head)(act)
 
         return 0
 
@@ -521,6 +570,7 @@
     value_side(HEADS - 1, 1)
     key_side(HEADS - 1, 1)
 
+    group_part(2)
     cot_t = [ref[...].reshape(C, PATCH).astype(BF16) for ref in (dqt_ref, dkt_ref, dvt_ref)]
     ng_t = dot(wqkv_ref[...], jnp.concatenate(cot_t, axis=0))
     for part in range(PARTS):
@@ -531,37 +581,41 @@
         mixed = jnp.mean(ng * xhat, axis=1, keepdims=True)
         grad = oga_ref[rows].astype(F32) + rstd_ref[rows] * (ng - ng_mean - xhat * mixed)
         start_part(grad, back_out, back_both, part, back_sems)
+        if part == 1:
+            group_scatter(2)
         if part:
             send_part(back_out, back_both, back_in, part - 1, CHIPS - STRIDE, back_sems)
     send_part(back_out, back_both, back_in, PARTS - 1, CHIPS - STRIDE, back_sems)
-    group_part(1)
-    group_half(1).start()
+    group_gather(2)
 
     at = at_ref[...].reshape(C, PATCH)
     block_out = x_ref[...].astype(F32) + dot(transposed(at), wp_ref[...])
     block_out = block_out.astype(BF16)
-    group_scatter(1)
+    group_finish(1)
     slot_col = as_column(recv_slots(hilbert_ref))
     gather = [gather_columns(slot_col, part) for part in range(PARTS)]
     out_ref[...] = dot(jnp.concatenate(gather, axis=1), block_out).astype(BF16)
     stores[0].start()
     group_close(0)
-    group_gather(1)
+    group_close(1)
     slot_col = as_column(send_slots(zorder_ref))
+    gather = [gather_columns(slot_col, part) for part in range(PARTS)]
+    group_finish(2)
     total = jnp.zeros((PATCH, C), F32)
     for part in range(PARTS):
-        gather = gather_columns(slot_col, part)
         wait_part(back_in, part, back_sems.at[3, part])
-        total += dot(gather, unpacked(back_in[part_chips(part)]))
+        total += dot(gather[part], unpacked(back_in[part_chips(part)]))
     feat_grad_ref[...] = total.astype(BF16)
     stores[1].start()
-    group_finish(1)
+    group_close(2)
+    for section in range(3):
+        qkvg_ref[:, section * C : (section + 1) * C] = assemble(section).T
+    projg_ref[...] = assemble(3)
+    stores[2].start()
+    stores[3].start()
     for part in range(PARTS):
         wait_part(there_in, part, there_sems.at[2, part])
         wait_part(back_in, part, back_sems.at[2, part])
-    group_close(1)
-    stores[2].start()
-    stores[3].start()
     for store in stores:
         store.wait()
 

time: 109 us -> 106 us (0.972)
  Pallas kernels: 108 us -> 105 us
    pallas_call x1, Pallas kernels: 105 us -> 103 us  [on_device(): pl.pallas_call(block_kernel, out_shape=out_shape, in_specs=[anywhere] * 6...]
where the time goes in v5:
time: 106 us
  Pallas kernels  105 us (99%)
    pallas_call x1, Pallas kernels, on_device(): pl.pallas_call(block_kernel, out_shape=out_shape, in_specs=[anywhere] * 6...  103 us
    pallas_call x1, Pallas kernels, on_device(): pl.pallas_call(finish_kernel, out_shape=out_shape, in_specs=[anywhere] *...  2.48 us

profile of v5, /device:TPU:1, one launch (start us, length us, event | category | flops | bytes accessed | tf_op | source)
XLA Modules:
  0.0 106.0 jit_solution(15651723791978974373)
XLA Ops:
  0.6 102.7 %shard_map.93 = (bf16[1024,256]{1,0:T(8,128)(2,1)}, bf16[1024,256]{1,0:T(8,128)(2,1)}, f32[256,768]{1,0:T(8,128)}, f32[256,256]{1,0:T(8,128)}) custom-call(bf16[1024,256]{1,0:T(8,128)(2,1)} %feat_hbm.1, s32[1,1024]{1,0:T(1,128)} %bitcast.2, s32[1,1024]{1,0:T(1,128)} %bitcast.3, bf16[256,768]{1,0:T(8,128)(2,1)} %wqkv_hbm.1, bf16[256,256]{1,0:T(8,128)(2,1)} %wp_hbm.1, ...), custom_call_target="tpu_custom_call" | custom-call | flops 28000000000 | bytes 5000000 | tf_op jit(solution)/shard_map/pallas_call | solution.py:659
  103.3 2.5 %shard_map.94 = (bf16[1024,256]{1,0:T(8,128)(2,1)}, bf16[1024,256]{1,0:T(8,128)(2,1)}, f32[256,768]{1,0:T(8,128)}, f32[256,256]{1,0:T(8,128)}) custom-call(bf16[1024,256]{1,0:T(8,128)(2,1)} %get-tuple-element.8.refs_0_, bf16[1024,256]{1,0:T(8,128)(2,1)} %get-tuple-element.9.refs_1_, f32[256,768]{1,0:T(8,128)} %get-tuple-element.10.refs_2_, ...), custom_call_target="tpu_custom_call" | custom-call | bytes 4000000 | tf_op jit(solution)/shard_map/pallas_call | solution.py:706

commit v6 on v5

--- a/solution.py
+++ b/solution.py
@@ -14,7 +14,7 @@
 QB = 512
 CHUNK = 64
 CHUNKS = PATCH // CHUNK
-STRIP = 256
+STRIP = 512
 EXP_SCALE = 0.25 * 1.4426950408889634
 
 F32 = jnp.float32

time: 106 us -> 107 us (level)
  no operation moved by 1% of the time
where the time goes in v6:
time: 107 us; the launch traced here: 106 us
  Pallas kernels  106 us (99%)
    pallas_call x1, Pallas kernels, on_device(): pl.pallas_call(block_kernel, out_shape=out_shape, in_specs=[anywhere] * 6...  103 us
    pallas_call x1, Pallas kernels, on_device(): pl.pallas_call(finish_kernel, out_shape=out_shape, in_specs=[anywhere] *...  2.48 us

profile of v6, /device:TPU:1, one launch (start us, length us, event | category | flops | bytes accessed | tf_op | source)
XLA Modules:
  0.0 106.4 jit_solution(12683180593565079152)
XLA Ops:
  0.6 103.1 %shard_map.93 = (bf16[1024,256]{1,0:T(8,128)(2,1)}, bf16[1024,256]{1,0:T(8,128)(2,1)}, f32[256,768]{1,0:T(8,128)}, f32[256,256]{1,0:T(8,128)}) custom-call(bf16[1024,256]{1,0:T(8,128)(2,1)} %feat_hbm.1, s32[1,1024]{1,0:T(1,128)} %bitcast.2, s32[1,1024]{1,0:T(1,128)} %bitcast.3, bf16[256,768]{1,0:T(8,128)(2,1)} %wqkv_hbm.1, bf16[256,256]{1,0:T(8,128)(2,1)} %wp_hbm.1, ...), custom_call_target="tpu_custom_call" | custom-call | flops 28000000000 | bytes 5000000 | tf_op jit(solution)/shard_map/pallas_call | solution.py:659
  103.7 2.5 %shard_map.94 = (bf16[1024,256]{1,0:T(8,128)(2,1)}, bf16[1024,256]{1,0:T(8,128)(2,1)}, f32[256,768]{1,0:T(8,128)}, f32[256,256]{1,0:T(8,128)}) custom-call(bf16[1024,256]{1,0:T(8,128)(2,1)} %get-tuple-element.8.refs_0_, bf16[1024,256]{1,0:T(8,128)(2,1)} %get-tuple-element.9.refs_1_, f32[256,768]{1,0:T(8,128)} %get-tuple-element.10.refs_2_, ...), custom_call_target="tpu_custom_call" | custom-call | bytes 4000000 | tf_op jit(solution)/shard_map/pallas_call | solution.py:706

commit v7 on v5

--- a/solution.py
+++ b/solution.py
@@ -206,7 +206,7 @@
 
 SIDE = 8
 GROUPS = 3
-FIRST_HEAD = (0, 8, 13, HEADS)
+FIRST_HEAD = (0, 8, 14, HEADS)
 OWNER_STRIDE = 13
 OWNER_INVERSE = 5
 
@@ -237,7 +237,7 @@
     out_ref, feat_grad_ref, qkvg_ref, projg_ref,
     feat_ref, zorder_ref, hilbert_ref, wqkv_ref, wp_ref, og_ref, oga_ref, x_ref, normed_ref,
     wqkv_t_ref, xhat_ref, rstd_ref, k_ref, v_ref, qt_ref, kt_ref, vt_ref, dot_ref,
-    p_ref, ds_ref, e_ref, at_ref, dqt_ref, dkt_ref, dvt_ref,
+    p_ref, ds_ref, rhs_ref, e_ref, at_ref, dqt_ref, dkt_ref, dvt_ref,
     there_out, there_both, there_in, back_out, back_both, back_in,
     part_ref, half_ref, sum_ref, chunk_in_ref, result_ref, total_ref, low_out_ref, low_in_ref,
     load_sems, there_sems, back_sems, group_sems, level_sems, store_sems,
@@ -503,7 +503,6 @@
         half = h // 8
         ql = slice(block * QB, (block + 1) * QB)
         qt = qt_ref[pl.ds(half * 8, 8), :, ql].reshape(half_width, QB)
-        dot_t = dot_ref[pl.ds(half * 8, 8), :, ql].reshape(half_width, QB)
         tops, sums = [], []
         for j in range(PATCH // STRIP):
             s = dot(km[j * STRIP : (j + 1) * STRIP], qt)
@@ -529,24 +528,30 @@
         key_side(before, 1 - block)
         at_ref[h, :, ql] = ot.astype(BF16)
         delta = jnp.sum(ot * dot_ref[h, :, ql].astype(F32), axis=0, keepdims=True)
+        pieces = []
+        for _ in range(3):
+            pieces.append(delta.astype(BF16).astype(F32))
+            delta = delta - pieces[-1]
+        pieces.append(jnp.zeros((HEAD_DIM - 3, QB), F32))
+        rhs_ref[block] = dot_ref[pl.ds(half * 8, 8), :, ql]
+        rhs_ref[block, lax.rem(h + 1, 8)] = jnp.concatenate(pieces, axis=0).astype(BF16)
+        dot_t = rhs_ref[block].reshape(half_width, QB)
         for j in range(PATCH // STRIP):
             dp = dot(vm[j * STRIP : (j + 1) * STRIP], dot_t)
             for c in range(STRIP // CHUNK):
                 rows = slice(j * STRIP + c * CHUNK, j * STRIP + (c + 1) * CHUNK)
                 p = p_ref[block, rows].astype(F32)
-                ds = p * (dp[c * CHUNK : (c + 1) * CHUNK] - delta)
+                ds = p * dp[c * CHUNK : (c + 1) * CHUNK]
                 ds_ref[block, rows] = ds.astype(BF16)
-
-    def after_scatter():
-        gather_done()
-        group_scatter(1)
 
     def head_step(h, _):
         half = h // 8
-        lane = lax.broadcasted_iota(jnp.int32, (1, half_width), 1) // HEAD_DIM
-        mask = (lane == h % 8).astype(F32).astype(BF16)
+        lane = lax.broadcasted_iota(jnp.int32, (1, half_width), 1)
+        mask = (lane // HEAD_DIM == h % 8).astype(F32).astype(BF16)
+        beyond = lane - (h + 1) % 8 * HEAD_DIM
+        minus = -((beyond >= 0) & (beyond < 3)).astype(F32).astype(BF16)
         km = k_ref[half] * mask
-        vm = v_ref[half] * mask
+        vm = v_ref[half] * mask + minus
         block_step(h, 0, km, vm, jnp.maximum(h - 1, 0))
         block_step(h, 1, km, vm, h)
 
@@ -556,9 +561,8 @@
             FIRST_HEAD[1] + 2: scatter_low,
             FIRST_HEAD[1] + 3: gather_low,
             FIRST_HEAD[1] + 4: gather_high,
+            FIRST_HEAD[1] + 5: gather_done,
             FIRST_HEAD[2]: lambda: group_part(1),
-            FIRST_HEAD[2] + 1: after_scatter,
-            FIRST_HEAD[2] + 2: lambda: group_gather(1),
         }
         for head, act in steps.items():
             pl.when(h == head)(act)
@@ -571,6 +575,7 @@
     key_side(HEADS - 1, 1)
 
     group_part(2)
+    group_scatter(1)
     cot_t = [ref[...].reshape(C, PATCH).astype(BF16) for ref in (dqt_ref, dkt_ref, dvt_ref)]
     ng_t = dot(wqkv_ref[...], jnp.concatenate(cot_t, axis=0))
     for part in range(PARTS):
@@ -586,6 +591,7 @@
         if part:
             send_part(back_out, back_both, back_in, part - 1, CHIPS - STRIDE, back_sems)
     send_part(back_out, back_both, back_in, PARTS - 1, CHIPS - STRIDE, back_sems)
+    group_gather(1)
     group_gather(2)
 
     at = at_ref[...].reshape(C, PATCH)
@@ -674,6 +680,7 @@
             pltpu.VMEM((PATCH, 1), F32),
             halves, halves, heads_t, heads_t, heads_t, heads_t,
             queries, queries,
+            pltpu.VMEM((2, 8, HEAD_DIM, QB), BF16),
             pltpu.VMEM((2, CHUNKS, CHUNK // 8, 8, QB), F32),
             heads_t, heads_t, heads_f, heads_f,
             pieces, pieces, pieces, pieces, pieces, pieces,

time: 106 us -> 109 us (1.028)
  Pallas kernels: 105 us -> 108 us
    pallas_call x1, Pallas kernels: 103 us -> 105 us  [on_device(): pl.pallas_call(block_kernel, out_shape=out_shape, in_specs=[anywhere] * 6...]
where the time goes in v7:
time: 109 us
  Pallas kernels  108 us (99%)
    pallas_call x1, Pallas kernels, on_device(): pl.pallas_call(block_kernel, out_shape=out_shape, in_specs=[anywhere] * 6...  105 us
    pallas_call x1, Pallas kernels, on_device(): pl.pallas_call(finish_kernel, out_shape=out_shape, in_specs=[anywhere] *...  2.48 us

profile of v7, /device:TPU:1, one launch (start us, length us, event | category | flops | bytes accessed | tf_op | source)
XLA Modules:
  0.0 108.7 jit_solution(12356496418618730480)
XLA Ops:
  0.6 105.4 %shard_map.93 = (bf16[1024,256]{1,0:T(8,128)(2,1)}, bf16[1024,256]{1,0:T(8,128)(2,1)}, f32[256,768]{1,0:T(8,128)}, f32[256,256]{1,0:T(8,128)}) custom-call(bf16[1024,256]{1,0:T(8,128)(2,1)} %feat_hbm.1, s32[1,1024]{1,0:T(1,128)} %bitcast.2, s32[1,1024]{1,0:T(1,128)} %bitcast.3, bf16[256,768]{1,0:T(8,128)(2,1)} %wqkv_hbm.1, bf16[256,256]{1,0:T(8,128)(2,1)} %wp_hbm.1, ...), custom_call_target="tpu_custom_call" | custom-call | flops 28000000000 | bytes 5000000 | tf_op jit(solution)/shard_map/pallas_call | solution.py:665
  106.0 2.5 %shard_map.94 = (bf16[1024,256]{1,0:T(8,128)(2,1)}, bf16[1024,256]{1,0:T(8,128)(2,1)}, f32[256,768]{1,0:T(8,128)}, f32[256,256]{1,0:T(8,128)}) custom-call(bf16[1024,256]{1,0:T(8,128)(2,1)} %get-tuple-element.8.refs_0_, bf16[1024,256]{1,0:T(8,128)(2,1)} %get-tuple-element.9.refs_1_, f32[256,768]{1,0:T(8,128)} %get-tuple-element.10.refs_2_, ...), custom_call_target="tpu_custom_call" | custom-call | bytes 4000000 | tf_op jit(solution)/shard_map/pallas_call | solution.py:713

commit v8 on v5

--- a/solution.py
+++ b/solution.py
@@ -237,7 +237,7 @@
     out_ref, feat_grad_ref, qkvg_ref, projg_ref,
     feat_ref, zorder_ref, hilbert_ref, wqkv_ref, wp_ref, og_ref, oga_ref, x_ref, normed_ref,
     wqkv_t_ref, xhat_ref, rstd_ref, k_ref, v_ref, qt_ref, kt_ref, vt_ref, dot_ref,
-    p_ref, ds_ref, e_ref, at_ref, dqt_ref, dkt_ref, dvt_ref,
+    p_ref, ds_ref, pt_ref, dst_ref, e_ref, at_ref, dqt_ref, dkt_ref, dvt_ref,
     there_out, there_both, there_in, back_out, back_both, back_in,
     part_ref, half_ref, sum_ref, chunk_in_ref, result_ref, total_ref, low_out_ref, low_in_ref,
     load_sems, there_sems, back_sems, group_sems, level_sems, store_sems,
@@ -491,12 +491,12 @@
 
     def value_side(h, block):
         ql = slice(block * QB, (block + 1) * QB)
-        dv = dot_nt(dot_ref[h, :, ql], p_ref[block]) * 4.0
+        dv = dot(dot_ref[h, :, ql], pt_ref[...]) * 4.0
         dvt_ref[h] = dvt_ref[h] + dv if block else dv
 
     def key_side(h, block):
         ql = slice(block * QB, (block + 1) * QB)
-        dk = dot_nt(qt_ref[h, :, ql], ds_ref[block])
+        dk = dot(qt_ref[h, :, ql], dst_ref[...])
         dkt_ref[h] = dkt_ref[h] + dk if block else dk
 
     def block_step(h, block, km, vm, before):
@@ -504,6 +504,8 @@
         ql = slice(block * QB, (block + 1) * QB)
         qt = qt_ref[pl.ds(half * 8, 8), :, ql].reshape(half_width, QB)
         dot_t = dot_ref[pl.ds(half * 8, 8), :, ql].reshape(half_width, QB)
+        pt_ref[...] = p_ref[1 - block].T
+        dst_ref[...] = ds_ref[1 - block].T
         tops, sums = [], []
         for j in range(PATCH // STRIP):
             s = dot(km[j * STRIP : (j + 1) * STRIP], qt)
@@ -566,6 +568,8 @@
         return 0
 
     lax.fori_loop(0, HEADS, head_step, 0)
+    pt_ref[...] = p_ref[1].T
+    dst_ref[...] = ds_ref[1].T
     query_side(HEADS - 1, 1)
     value_side(HEADS - 1, 1)
     key_side(HEADS - 1, 1)
@@ -674,6 +678,8 @@
             pltpu.VMEM((PATCH, 1), F32),
             halves, halves, heads_t, heads_t, heads_t, heads_t,
             queries, queries,
+            pltpu.VMEM((QB, PATCH), BF16),
+            pltpu.VMEM((QB, PATCH), BF16),
             pltpu.VMEM((2, CHUNKS, CHUNK // 8, 8, QB), F32),
             heads_t, heads_t, heads_f, heads_f,
             pieces, pieces, pieces, pieces, pieces, pieces,

time: 106 us -> 107 us (level)
  no operation moved by 1% of the time
where the time goes in v8:
time: 107 us
  Pallas kernels  106 us (99%)
    pallas_call x1, Pallas kernels, on_device(): pl.pallas_call(block_kernel, out_shape=out_shape, in_specs=[anywhere] * 6...  104 us
    pallas_call x1, Pallas kernels, on_device(): pl.pallas_call(finish_kernel, out_shape=out_shape, in_specs=[anywhere] *...  2.48 us

profile of v8, /device:TPU:1, one launch (start us, length us, event | category | flops | bytes accessed | tf_op | source)
XLA Modules:
  0.0 106.8 jit_solution(15762301152221055876)
XLA Ops:
  0.6 103.5 %shard_map.93 = (bf16[1024,256]{1,0:T(8,128)(2,1)}, bf16[1024,256]{1,0:T(8,128)(2,1)}, f32[256,768]{1,0:T(8,128)}, f32[256,256]{1,0:T(8,128)}) custom-call(bf16[1024,256]{1,0:T(8,128)(2,1)} %feat_hbm.1, s32[1,1024]{1,0:T(1,128)} %bitcast.2, s32[1,1024]{1,0:T(1,128)} %bitcast.3, bf16[256,768]{1,0:T(8,128)(2,1)} %wqkv_hbm.1, bf16[256,256]{1,0:T(8,128)(2,1)} %wp_hbm.1, ...), custom_call_target="tpu_custom_call" | custom-call | flops 28000000000 | bytes 5000000 | tf_op jit(solution)/shard_map/pallas_call | solution.py:663
  104.1 2.5 %shard_map.94 = (bf16[1024,256]{1,0:T(8,128)(2,1)}, bf16[1024,256]{1,0:T(8,128)(2,1)}, f32[256,768]{1,0:T(8,128)}, f32[256,256]{1,0:T(8,128)}) custom-call(bf16[1024,256]{1,0:T(8,128)(2,1)} %get-tuple-element.8.refs_0_, bf16[1024,256]{1,0:T(8,128)(2,1)} %get-tuple-element.9.refs_1_, f32[256,768]{1,0:T(8,128)} %get-tuple-element.10.refs_2_, ...), custom_call_target="tpu_custom_call" | custom-call | bytes 4000000 | tf_op jit(solution)/shard_map/pallas_call | solution.py:712

commit v9 on v5

--- a/solution.py
+++ b/solution.py
@@ -11,8 +11,8 @@
 HEAD_DIM = 16
 PATCH = 1024
 C = 256
-QB = 512
-CHUNK = 64
+QB = 1024
+CHUNK = 32
 CHUNKS = PATCH // CHUNK
 STRIP = 256
 EXP_SCALE = 0.25 * 1.4426950408889634
@@ -286,8 +286,6 @@
     wqkv_t_ref[...] = transposed(wqkv_ref[...])
     p_ref[1] = jnp.zeros((PATCH, QB), BF16)
     ds_ref[1] = jnp.zeros((PATCH, QB), BF16)
-    dkt_ref[0] = jnp.zeros((HEAD_DIM, PATCH), F32)
-    dvt_ref[0] = jnp.zeros((HEAD_DIM, PATCH), F32)
 
     for part in range(PARTS):
         wait_part(there_in, part, there_sems.at[3, part])
@@ -485,23 +483,18 @@
             rows.append(untiled(total_ref[g, section // 2, low : low + half]))
         return jnp.concatenate(rows, axis=0)
 
-    def query_side(h, block):
-        ql = slice(block * QB, (block + 1) * QB)
-        dqt_ref[h, :, ql] = dot(kt_ref[h], ds_ref[block]).astype(BF16)
-
-    def value_side(h, block):
-        ql = slice(block * QB, (block + 1) * QB)
-        dv = dot_nt(dot_ref[h, :, ql], p_ref[block]) * 4.0
-        dvt_ref[h] = dvt_ref[h] + dv if block else dv
-
-    def key_side(h, block):
-        ql = slice(block * QB, (block + 1) * QB)
-        dk = dot_nt(qt_ref[h, :, ql], ds_ref[block])
-        dkt_ref[h] = dkt_ref[h] + dk if block else dk
+    def query_side(h, slot):
+        dqt_ref[h] = dot(kt_ref[h], ds_ref[slot]).astype(BF16)
+
+    def value_side(h, slot):
+        dvt_ref[h] = dot_nt(dot_ref[h], p_ref[slot]) * 4.0
+
+    def key_side(h, slot):
+        dkt_ref[h] = dot_nt(qt_ref[h], ds_ref[slot])
 
     def block_step(h, block, km, vm, before):
         half = h // 8
-        ql = slice(block * QB, (block + 1) * QB)
+        ql = slice(0, QB)
         qt = qt_ref[pl.ds(half * 8, 8), :, ql].reshape(half_width, QB)
         dot_t = dot_ref[pl.ds(half * 8, 8), :, ql].reshape(half_width, QB)
         tops, sums = [], []
@@ -541,15 +534,19 @@
         gather_done()
         group_scatter(1)
 
-    def head_step(h, _):
-        half = h // 8
-        lane = lax.broadcasted_iota(jnp.int32, (1, half_width), 1) // HEAD_DIM
-        mask = (lane == h % 8).astype(F32).astype(BF16)
-        km = k_ref[half] * mask
-        vm = v_ref[half] * mask
-        block_step(h, 0, km, vm, jnp.maximum(h - 1, 0))
-        block_step(h, 1, km, vm, h)
-
+    def head_step(pair, _):
+        for slot in range(2):
+            h = pair * 2 + slot
+            half = h // 8
+            lane = lax.broadcasted_iota(jnp.int32, (1, half_width), 1) // HEAD_DIM
+            mask = (lane == h % 8).astype(F32).astype(BF16)
+            km = k_ref[half] * mask
+            vm = v_ref[half] * mask
+            block_step(h, slot, km, vm, jnp.maximum(h - 1, 0))
+            group_steps(h, slot)
+        return 0
+
+    def group_steps(h, slot):
         steps = {
             FIRST_HEAD[1]: lambda: group_part(0),
             FIRST_HEAD[1] + 1: scatter_high,
@@ -561,11 +558,10 @@
             FIRST_HEAD[2] + 2: lambda: group_gather(1),
         }
         for head, act in steps.items():
-            pl.when(h == head)(act)
-
-        return 0
-
-    lax.fori_loop(0, HEADS, head_step, 0)
+            if head % 2 == slot:
+                pl.when(h == head)(act)
+
+    lax.fori_loop(0, HEADS // 2, head_step, 0)
     query_side(HEADS - 1, 1)
     value_side(HEADS - 1, 1)
     key_side(HEADS - 1, 1)

time: 106 us -> 112 us (1.057)
  Pallas kernels: 105 us -> 111 us
    pallas_call x1, Pallas kernels: 103 us -> 108 us  [on_device(): pl.pallas_call(block_kernel, out_shape=out_shape, in_specs=[anywhere] * 6...]
where the time goes in v9:
time: 112 us
  Pallas kernels  111 us (99%)
    pallas_call x1, Pallas kernels, on_device(): pl.pallas_call(block_kernel, out_shape=out_shape, in_specs=[anywhere] * 6...  108 us
    pallas_call x1, Pallas kernels, on_device(): pl.pallas_call(finish_kernel, out_shape=out_shape, in_specs=[anywhere] *...  2.48 us

profile of v9, /device:TPU:1, one launch (start us, length us, event | category | flops | bytes accessed | tf_op | source)
XLA Modules:
  0.0 111.8 jit_solution(13017786294283736312)
XLA Ops:
  0.6 108.5 %shard_map.93 = (bf16[1024,256]{1,0:T(8,128)(2,1)}, bf16[1024,256]{1,0:T(8,128)(2,1)}, f32[256,768]{1,0:T(8,128)}, f32[256,256]{1,0:T(8,128)}) custom-call(bf16[1024,256]{1,0:T(8,128)(2,1)} %feat_hbm.1, s32[1,1024]{1,0:T(1,128)} %bitcast.2, s32[1,1024]{1,0:T(1,128)} %bitcast.3, bf16[256,768]{1,0:T(8,128)(2,1)} %wqkv_hbm.1, bf16[256,256]{1,0:T(8,128)(2,1)} %wp_hbm.1, ...), custom_call_target="tpu_custom_call" | custom-call | flops 28000000000 | bytes 5000000 | tf_op jit(solution)/shard_map/pallas_call | solution.py:655
  109.1 2.5 %shard_map.94 = (bf16[1024,256]{1,0:T(8,128)(2,1)}, bf16[1024,256]{1,0:T(8,128)(2,1)}, f32[256,768]{1,0:T(8,128)}, f32[256,256]{1,0:T(8,128)}) custom-call(bf16[1024,256]{1,0:T(8,128)(2,1)} %get-tuple-element.8.refs_0_, bf16[1024,256]{1,0:T(8,128)(2,1)} %get-tuple-element.9.refs_1_, f32[256,768]{1,0:T(8,128)} %get-tuple-element.10.refs_2_, ...), custom_call_target="tpu_custom_call" | custom-call | bytes 4000000 | tf_op jit(solution)/shard_map/pallas_call | solution.py:702

commit v10 on v5

--- a/solution.py
+++ b/solution.py
@@ -13,7 +13,7 @@
 C = 256
 QB = 512
 CHUNK = 64
-CHUNKS = PATCH // CHUNK
+TALL = 128
 STRIP = 256
 EXP_SCALE = 0.25 * 1.4426950408889634
 
@@ -504,27 +504,35 @@
         ql = slice(block * QB, (block + 1) * QB)
         qt = qt_ref[pl.ds(half * 8, 8), :, ql].reshape(half_width, QB)
         dot_t = dot_ref[pl.ds(half * 8, 8), :, ql].reshape(half_width, QB)
-        tops, sums = [], []
+        tops, sums = ([], []), ([], [])
         for j in range(PATCH // STRIP):
             s = dot(km[j * STRIP : (j + 1) * STRIP], qt)
             if j == 0:
                 query_side(before, 1 - block)
-            for c in range(STRIP // CHUNK):
-                part = s[c * CHUNK : (c + 1) * CHUNK].reshape(CHUNK // 8, 8, QB)
-                top = jnp.max(part, axis=0)
-                e = jnp.exp2((part - top) * EXP_SCALE)
-                e_ref[block, j * (STRIP // CHUNK) + c] = e
-                tops.append(top)
-                sums.append(jnp.sum(e, axis=0))
+            for c in range(STRIP // TALL):
+                for g in range(2):
+                    lanes = slice(g * QB // 2, (g + 1) * QB // 2)
+                    part = s[c * TALL : (c + 1) * TALL, lanes].reshape(TALL // 8, 8, QB // 2)
+                    top = jnp.max(part, axis=0)
+                    e = jnp.exp2((part - top) * EXP_SCALE)
+                    e_ref[block, j * (STRIP // TALL) + c, :, :, lanes] = e
+                    tops[g].append(top)
+                    sums[g].append(jnp.sum(e, axis=0))
         value_side(before, 1 - block)
-        peak = functools.reduce(jnp.maximum, tops)
-        peak = jnp.max(peak, axis=0, keepdims=True)
-        weights = [jnp.exp2((top - peak) * EXP_SCALE) for top in tops]
-        total = functools.reduce(jnp.add, [a * w for a, w in zip(sums, weights)])
-        inverse = 1.0 / jnp.sum(total, axis=0, keepdims=True)
-        for c in range(CHUNKS):
-            p = e_ref[block, c] * (weights[c] * inverse)
-            p_ref[block, c * CHUNK : (c + 1) * CHUNK] = p.reshape(CHUNK, QB).astype(BF16)
+        weights = []
+        for g in range(2):
+            peak = functools.reduce(jnp.maximum, tops[g])
+            peak = jnp.max(peak, axis=0, keepdims=True)
+            scales = [jnp.exp2((top - peak) * EXP_SCALE) for top in tops[g]]
+            total = functools.reduce(jnp.add, [a * w for a, w in zip(sums[g], scales)])
+            inverse = 1.0 / jnp.sum(total, axis=0, keepdims=True)
+            weights.append([scale * inverse for scale in scales])
+        for c in range(PATCH // TALL):
+            for g in range(2):
+                lanes = slice(g * QB // 2, (g + 1) * QB // 2)
+                p = e_ref[block, c, :, :, lanes] * weights[g][c]
+                rows = slice(c * TALL, (c + 1) * TALL)
+                p_ref[block, rows, lanes] = p.reshape(TALL, QB // 2).astype(BF16)
         ot = dot(vt_ref[h], p_ref[block])
         key_side(before, 1 - block)
         at_ref[h, :, ql] = ot.astype(BF16)
@@ -674,7 +682,7 @@
             pltpu.VMEM((PATCH, 1), F32),
             halves, halves, heads_t, heads_t, heads_t, heads_t,
             queries, queries,
-            pltpu.VMEM((2, CHUNKS, CHUNK // 8, 8, QB), F32),
+            pltpu.VMEM((2, PATCH // TALL, TALL // 8, 8, QB), F32),
             heads_t, heads_t, heads_f, heads_f,
             pieces, pieces, pieces, pieces, pieces, pieces,
             both_cores, one_core, one_core, one_core,

time: 106 us -> 108 us (1.019)
  Pallas kernels: 105 us -> 107 us
    pallas_call x1, Pallas kernels: 103 us -> 104 us  [on_device(): pl.pallas_call(block_kernel, out_shape=out_shape, in_specs=[anywhere] * 6...]
where the time goes in v10:
time: 108 us; the launch traced here: 107 us
  Pallas kernels  107 us (99%)
    pallas_call x1, Pallas kernels, on_device(): pl.pallas_call(block_kernel, out_shape=out_shape, in_specs=[anywhere] * 6...  104 us
    pallas_call x1, Pallas kernels, on_device(): pl.pallas_call(finish_kernel, out_shape=out_shape, in_specs=[anywhere] *...  2.48 us

profile of v10, /device:TPU:1, one launch (start us, length us, event | category | flops | bytes accessed | tf_op | source)
XLA Modules:
  0.0 107.5 jit_solution(12881477576990333225)
XLA Ops:
  0.6 104.2 %shard_map.93 = (bf16[1024,256]{1,0:T(8,128)(2,1)}, bf16[1024,256]{1,0:T(8,128)(2,1)}, f32[256,768]{1,0:T(8,128)}, f32[256,256]{1,0:T(8,128)}) custom-call(bf16[1024,256]{1,0:T(8,128)(2,1)} %feat_hbm.1, s32[1,1024]{1,0:T(1,128)} %bitcast.2, s32[1,1024]{1,0:T(1,128)} %bitcast.3, bf16[256,768]{1,0:T(8,128)(2,1)} %wqkv_hbm.1, bf16[256,256]{1,0:T(8,128)(2,1)} %wp_hbm.1, ...), custom_call_target="tpu_custom_call" | custom-call | flops 28000000000 | bytes 5000000 | tf_op jit(solution)/shard_map/pallas_call | solution.py:667
  104.8 2.5 %shard_map.94 = (bf16[1024,256]{1,0:T(8,128)(2,1)}, bf16[1024,256]{1,0:T(8,128)(2,1)}, f32[256,768]{1,0:T(8,128)}, f32[256,256]{1,0:T(8,128)}) custom-call(bf16[1024,256]{1,0:T(8,128)(2,1)} %get-tuple-element.8.refs_0_, bf16[1024,256]{1,0:T(8,128)(2,1)} %get-tuple-element.9.refs_1_, f32[256,768]{1,0:T(8,128)} %get-tuple-element.10.refs_2_, ...), custom_call_target="tpu_custom_call" | custom-call | bytes 4000000 | tf_op jit(solution)/shard_map/pallas_call | solution.py:714
